TPU v7x, 512 devices: a whole 4x4x16 slice. The times are simulated.
512 devices in a mesh: dp: 32 (over x, y, core), vocab: 16 (over z).
Axes of the slice: x: 4, y: 4, z: 16, core: 2. Of those that a mesh axis runs over, the one named last changes fastest.
Arguments:
- hidden: float32 [64, 4608], P('dp'), may hold values from -6 to 6
- norm_gain: float32 [4608], replicated, may hold values from 0.5 to 1.5
- embed_table: bfloat16 [196608, 4608], P(('dp', 'vocab')), as said below
- tokens: int32 [64, 3], replicated, may hold values from 0 to 196607, as said below
Outputs:
- log_probs: float32 [64, 3], P('dp')
- final_hidden: float32 [64, 4608], P('dp')
Inputs may be any that keep to these rules, and one draw needn't show every extreme that they name: `tokens`: token ids are vocabulary entries. `embed_table`: entries lie between -21 / sqrt(4608) and 21 / sqrt(4608).
All inputs are finite; a program needn't handle non-finite values.
Results may differ from a plain program's by a relative error of at most 0.0003.
Values may be sent and summed in bfloat16 or wider, within the bound.
No kernel may reach another device: no remote copies, remote signals or barrier semaphores. Data moves between devices by JAX's collectives and lax.ppermute only.
A program may use at most 64 MiB of HBM per device.

v0:
```python
import functools
import math

import jax
import jax.numpy as jnp
from jax import lax
from jax.sharding import Mesh
from jax.sharding import PartitionSpec as P

D = 4608
STEPS = 3
DP = ("dp_0", "dp_1", "dp_2")
DP_VOCAB = ("dp_0", "dp_1", "dp_2", "vocab")


epsilon_value = 1e-06
softcap_value = 30.0


def in_blocks(x, dim, size):
    lengths = x.shape
    blocks = x.reshape(*lengths[:dim], size, lengths[dim] // size, *lengths[dim + 1 :])
    return jnp.moveaxis(blocks, dim, 0)


def sum_at_owner(x, axis, dim):
    blocks = in_blocks(x, dim, lax.axis_size(axis))
    arrived = lax.all_to_all(blocks, axis, split_axis=0, concat_axis=0, tiled=True)
    return arrived.astype(jnp.float32).sum(axis=0)


def copy_for_each(x, axis):
    size = lax.axis_size(axis)
    return lax.all_to_all(jnp.broadcast_to(x[None], (size, *x.shape)), axis, 0, 0, tiled=True)


def of_everyone(x, axis):
    return copy_for_each(x, axis).astype(jnp.float32).sum(axis=0)


def joined_along(blocks, dim):
    blocks = jnp.moveaxis(blocks, 0, dim)
    lengths = blocks.shape
    return blocks.reshape(*lengths[:dim], lengths[dim] * lengths[dim + 1], *lengths[dim + 2 :])


def gathered_copies(x, axis, dim):
    blocks = copy_for_each(x, axis)
    return joined_along(blocks, dim)


def over_axes(x, axes):
    return functools.reduce(lax.psum, axes, x)


def project_rows(normed, embed_table):
    return lax.dot_general(
        normed, embed_table, (((1,), (1,)), ((), ())), preferred_element_type=jnp.float32
    )


def on_device(hidden, norm_gain, embed_table, tokens):
    own_rows = hidden.shape[0]
    shard_rows = embed_table.shape[0]
    own_start = lax.axis_index(DP) * own_rows
    shard_start = (
        lax.axis_index(DP) * lax.axis_size("vocab") + lax.axis_index("vocab")
    ) * shard_rows
    scale_factor = math.sqrt(D)
    local_ids = jnp.transpose(tokens) - shard_start
    columns = lax.broadcasted_iota(jnp.int32, (1, 1, shard_rows), 2)
    matches = local_ids[:, :, None] == columns
    onehot = matches.astype(jnp.bfloat16)
    found = jnp.einsum("sbv,vd->sbd", onehot, embed_table, preferred_element_type=jnp.float32)
    current = hidden
    partial_value = sum_at_owner(found.astype(jnp.bfloat16), DP, 1)
    summed = of_everyone(partial_value.astype(jnp.bfloat16), "vocab").astype(jnp.float32)
    results = []
    for decode_step in range(STEPS):
        square_mean = jnp.mean(current * current, axis=-1, keepdims=True)
        normed = (current * lax.rsqrt(square_mean + epsilon_value) * norm_gain).astype(jnp.bfloat16)
        logits = project_rows(gathered_copies(normed, DP, 0), embed_table)
        capped = softcap_value * jnp.tanh(logits / softcap_value)
        exp_total = jnp.sum(jnp.exp(capped), axis=-1)
        target = jnp.sum(jnp.where(matches[decode_step], capped, 0.0), axis=-1)
        exp_total, target = (over_axes(exp_total, DP_VOCAB), over_axes(target, DP_VOCAB))
        exp_total = lax.dynamic_slice_in_dim(exp_total, own_start, own_rows, 0)
        target = lax.dynamic_slice_in_dim(target, own_start, own_rows, 0)
        results.append(target - jnp.log(exp_total))
        current = current + scale_factor * summed[decode_step]
    return (jnp.stack(results, axis=1), current)


def solution(mesh):
    finer = Mesh(
        mesh.devices.reshape(4, 4, 2, mesh.shape["vocab"]), ("dp_0", "dp_1", "dp_2", "vocab")
    )
    in_specs = (P(DP, None), P(), P(DP_VOCAB, None), P())
    out_specs = (P(DP, None), P(DP, None))
    return jax.shard_map(
        on_device, mesh=finer, in_specs=in_specs, out_specs=out_specs, check_vma=False
    )
```

profile of v0, /device:TPU:2, one launch (start us, length us, event | category | flops | bytes accessed | tf_op | source)
XLA Modules:
  0.0 223.4 jit_solution(6400162079562616659)
XLA Ops:
  0.6 0.0 copy-start
  0.7 0.8 subtract_bitcast_fusion
  1.5 1.2 copy-done
  2.7 2.3 %convolution_convert_fusion = bf16[3,64,4608]{2,1,0:T(8,128)(2,1)} fusion(bf16[384,4608]{1,0:T(8,128)(2,1)S(1)} %copy-done, s32[3,64]{1,0:T(4,128)S(1)} %subtract_bitcast_fusion), kind=kOutput, calls=%fused_computation | convolution fusion | flops 680435712 | bytes 5309184 | tf_op jit(solution)/shard_map/sbv,vd->sbd/dot_general | solution.py:74
  5.0 3.8 %reshape.53 = bf16[3,32,2,4608]{3,2,1,0:T(2,128)(2,1)} reshape(bf16[3,64,4608]{2,1,0:T(8,128)(2,1)} %convolution_convert_fusion) | data formatting | bytes 3538944 | tf_op jit(solution)/shard_map/reshape | solution.py:22
  8.8 2.7 %copy.19 = bf16[3,32,2,4608]{3,2,0,1:T(2,128)(2,1)S(1)} copy(bf16[3,32,2,4608]{3,2,1,0:T(2,128)(2,1)} %reshape.53) | data formatting | bytes 3538944 | tf_op jit(solution)/shard_map/reshape | solution.py:22
  11.5 32.1 %all_to_all.25 = bf16[32,3,2,4608]{3,2,1,0:T(2,128)(2,1)} all-to-all(bf16[32,3,2,4608]{3,2,1,0:T(2,128)(2,1)S(1)} %bitcast.46), channel_id=1, replica_groups=mesh['dp_0'=4,'dp_1'=4,'dp_2'=2,'vocab'=16] {'dp_0','dp_1','dp_2'}, dimensions={0} | all-to-all | bytes 3538944 | tf_op jit(solution)/shard_map/all_to_all | solution.py:28
  43.6 3.6 %reduce_sum.105 = bf16[3,2,4608]{2,1,0:T(2,128)(2,1)} reduce(bf16[32,3,2,4608]{3,2,1,0:T(2,128)(2,1)} %all_to_all.25, bf16[]{:T(256)} %constant.48.clone.1), dimensions={0}, to_apply=%region_11.12 | reduce | flops 857088 | bytes 1824770 | tf_op jit(solution)/shard_map/reduce_sum | solution.py:29
  47.1 0.0 copy-start.2
  47.1 0.0 copy-start.3
  47.1 1.3 broadcast_in_dim.16
  48.4 59.2 %all_to_all.26 = bf16[16,3,2,4608]{3,2,1,0:T(2,128)(2,1)S(1)} all-to-all(bf16[16,3,2,4608]{3,2,1,0:T(2,128)(2,1)S(1)} %broadcast_in_dim.16), channel_id=1, replica_groups=mesh['dp_0'=4,'dp_1'=4,'dp_2'=2,'vocab'=16] {'vocab'}, dimensions={0} | all-to-all | bytes 1769472 | tf_op jit(solution)/shard_map/all_to_all | solution.py:34
  107.6 0.3 convert_reduce_fusion
  107.9 0.0 copy-done.2
  107.9 0.8 fusion.8
  108.7 0.2 multiply_reduce_fusion
  108.9 0.0 copy-done.3
  109.0 0.7 multiply_convert_fusion.1
  109.7 0.3 broadcast_in_dim.17
  110.0 15.9 %all_to_all.27 = bf16[32,2,4608]{2,1,0:T(2,128)(2,1)} all-to-all(bf16[32,2,4608]{2,1,0:T(2,128)(2,1)S(1)} %broadcast_in_dim.17), channel_id=1, replica_groups=mesh['dp_0'=4,'dp_1'=4,'dp_2'=2,'vocab'=16] {'dp_0','dp_1','dp_2'}, dimensions={0} | all-to-all | bytes 1179648 | tf_op jit(solution)/shard_map/all_to_all | solution.py:34
  125.9 1.1 broadcast_in_dim.18
  127.0 6.1 %all-to-all-start.4 = ((bf16[32,2,4608]{2,1,0:T(2,128)(2,1)}), bf16[32,2,4608]{2,1,0:T(2,128)(2,1)}, u32[]{:S(2)}, u32[]{:S(2)}) async-start(bf16[32,2,4608]{2,1,0:T(2,128)(2,1)} %broadcast_in_dim.18), calls=%async_computation.4 | async-start | bytes 1179648 | tf_op jit(solution)/shard_map/all_to_all | solution.py:34
  133.1 0.7 iota_compare_fusion
  133.9 2.1 reshape.54
  136.0 7.5 %all-to-all-done.4 = bf16[32,2,4608]{2,1,0:T(2,128)(2,1)} async-done(((bf16[32,2,4608]{2,1,0:T(2,128)(2,1)}), bf16[32,2,4608]{2,1,0:T(2,128)(2,1)}, u32[]{:S(2)}, u32[]{:S(2)}) %all-to-all-start.4) | async-done | bytes 589856 | tf_op jit(solution)/shard_map/all_to_all | solution.py:34
  143.5 1.9 broadcast_in_dim.14
  145.3 6.0 %all-to-all-start = ((bf16[32,2,4608]{2,1,0:T(2,128)(2,1)}), bf16[32,2,4608]{2,1,0:T(2,128)(2,1)}, u32[]{:S(2)}, u32[]{:S(2)}) async-start(bf16[32,2,4608]{2,1,0:T(2,128)(2,1)} %broadcast_in_dim.14), calls=%async_computation | async-start | bytes 1179648 | tf_op jit(solution)/shard_map/all_to_all | solution.py:34
  151.4 2.1 reshape.55
  153.5 0.0 copy-start.1
  153.5 3.0 %fusion.5 = f32[64,384]{1,0:T(8,128)} fusion(bf16[64,4608]{1,0:T(8,128)(2,1)} %reshape.54, bf16[384,4608]{1,0:T(8,128)(2,1)S(1)} %copy-done), kind=kOutput, calls=%fused_computation.11 | convolution fusion | flops 226541568 | bytes 4227072 | tf_op jit(solution)/shard_map/dot_general | solution.py:57
  156.4 0.0 copy-done.1
  156.4 1.8 fusion.6
  158.3 3.4 %all-to-all-done = bf16[32,2,4608]{2,1,0:T(2,128)(2,1)} async-done(((bf16[32,2,4608]{2,1,0:T(2,128)(2,1)}), bf16[32,2,4608]{2,1,0:T(2,128)(2,1)}, u32[]{:S(2)}, u32[]{:S(2)}) %all-to-all-start) | async-done | bytes 589856 | tf_op jit(solution)/shard_map/all_to_all | solution.py:34
  161.7 2.1 reshape.52
  163.8 3.3 %select_reduce_fusion.2 = (f32[64]{0:T(128)S(1)}, f32[64]{0:T(128)S(1)}, f32[64]{0:T(128)S(1)}, f32[64]{0:T(128)S(1)}, f32[64]{0:T(128)}, /*index=5*/f32[64]{0:T(128)}) fusion(pred[3,64,384]{2,1,0:T(32,128)(4,1)} %iota_compare_fusion, f32[64,384]{1,0:T(8,128)} %fusion.6, f32[64,384]{1,0:T(8,128)} %fusion.5, bf16[64,4608]{1,0:T(8,128)(2,1)} %reshape.52, ...), kind=kOutput, calls=%fused_computation.19 | convolution fusion | flops 226762368 | bytes 4400640 | tf_op jit(solution)/shard_map/dot_general | solution.py:57
  167.1 10.2 %all-reduce.2 = (f32[64]{0:T(128)}, f32[64]{0:T(128)}, f32[64]{0:T(128)}, f32[64]{0:T(128)}, f32[64]{0:T(128)}, /*index=5*/f32[64]{0:T(128)}) all-reduce(f32[64]{0:T(128)S(1)} %get-tuple-element.18, f32[64]{0:T(128)S(1)} %get-tuple-element.19, ...), channel_id=1, replica_groups=mesh['dp_0'=4,'dp_1'=4,'dp_2'=2,'vocab'=16] {'dp_0'}, use_global_device_ids=true, to_apply=%region_31.32 | all-reduce | flops 384 | bytes 3072 | tf_op jit(solution)/shard_map/psum | solution.py:53
  177.3 10.1 %all-reduce.1 = (f32[64]{0:T(128)S(1)}, f32[64]{0:T(128)S(1)}, f32[64]{0:T(128)S(1)}, f32[64]{0:T(128)S(1)}, f32[64]{0:T(128)}, /*index=5*/f32[64]{0:T(128)}) all-reduce(f32[64]{0:T(128)} %get-tuple-element.34, f32[64]{0:T(128)} %get-tuple-element.35, ...), channel_id=1, replica_groups=mesh['dp_0'=4,'dp_1'=4,'dp_2'=2,'vocab'=16] {'dp_1'}, use_global_device_ids=true, to_apply=%region_32.33 | all-reduce | flops 384 | bytes 3072 | tf_op jit(solution)/shard_map/psum | solution.py:53
  187.3 3.2 %all-reduce.3 = (f32[64]{0:T(128)}, f32[64]{0:T(128)}, f32[64]{0:T(128)}, f32[64]{0:T(128)}, f32[64]{0:T(128)}, /*index=5*/f32[64]{0:T(128)}) all-reduce(f32[64]{0:T(128)S(1)} %get-tuple-element.28, f32[64]{0:T(128)S(1)} %get-tuple-element.29, ...), channel_id=1, replica_groups=mesh['dp_0'=4,'dp_1'=4,'dp_2'=2,'vocab'=16] {'dp_2'}, use_global_device_ids=true, to_apply=%region_33.34 | all-reduce | flops 384 | bytes 3072 | tf_op jit(solution)/shard_map/psum | solution.py:53
  190.5 31.4 %all-reduce = (f32[64]{0:T(128)S(1)}, f32[64]{0:T(128)S(1)}, f32[64]{0:T(128)S(1)}, f32[64]{0:T(128)S(1)}, f32[64]{0:T(128)}, /*index=5*/f32[64]{0:T(128)}) all-reduce(f32[64]{0:T(128)} %get-tuple-element.40, f32[64]{0:T(128)} %get-tuple-element.41, ...), channel_id=1, replica_groups=mesh['dp_0'=4,'dp_1'=4,'dp_2'=2,'vocab'=16] {'vocab'}, use_global_device_ids=true, to_apply=%region_34.35 | all-reduce | flops 384 | bytes 3072 | tf_op jit(solution)/shard_map/psum | solution.py:53
  221.8 0.8 subtract_bitcast_fusion.3
  222.6 0.1 subtract_bitcast_fusion.2
  222.7 0.1 subtract_bitcast_fusion.1
  222.8 0.7 copy.16
  (4 shorter events, 0.0 us)
Async XLA Ops:
  0.6 2.0 copy-start
  47.1 60.8 %copy-start.2 = (f32[2,4608]{1,0:T(2,128)S(1)}, f32[2,4608]{1,0:T(2,128)}, u32[]{:S(2)}) copy-start(f32[2,4608]{1,0:T(2,128)} %param.4) | copy-start | bytes 110596
  47.1 61.8 %copy-start.3 = (f32[4608]{0:T(1024)S(1)}, f32[4608]{0:T(1024)}, u32[]{:S(2)}) copy-start(f32[4608]{0:T(1024)} %param.5) | copy-start | bytes 55300
  127.0 16.4 %all-to-all-start.4 = ((bf16[32,2,4608]{2,1,0:T(2,128)(2,1)}), bf16[32,2,4608]{2,1,0:T(2,128)(2,1)}, u32[]{:S(2)}, u32[]{:S(2)}) async-start(bf16[32,2,4608]{2,1,0:T(2,128)(2,1)} %broadcast_in_dim.18), calls=%async_computation.4 | async-start | bytes 1179648 | tf_op jit(solution)/shard_map/all_to_all | solution.py:34
  145.3 16.4 %all-to-all-start = ((bf16[32,2,4608]{2,1,0:T(2,128)(2,1)}), bf16[32,2,4608]{2,1,0:T(2,128)(2,1)}, u32[]{:S(2)}, u32[]{:S(2)}) async-start(bf16[32,2,4608]{2,1,0:T(2,128)(2,1)} %broadcast_in_dim.14), calls=%async_computation | async-start | bytes 1179648 | tf_op jit(solution)/shard_map/all_to_all | solution.py:34
  153.5 3.0 %copy-start.1 = (bf16[64,4608]{1,0:T(8,128)(2,1)S(1)}, bf16[64,4608]{1,0:T(8,128)(2,1)}, u32[]{:S(2)}) copy-start(bf16[64,4608]{1,0:T(8,128)(2,1)} %reshape.55) | copy-start | bytes 1769476
where the time goes:
time: 224 us; the launch traced here: 223 us
  blocking collectives  162 us (72%)
  local copies, waits for them, and re-layouts  19.2 us (9%)
  starting transfers between devices  12.1 us (5%)
  waiting for transfers between devices  10.8 us (5%)
  matrix products  10.4 us (5%)
  other arithmetic  8.08 us (4%)
    all_to_all x2, blocking collectives, copy_for_each(): lax.all_to_all(jnp.broadcast_to(x[None], (size, *x.shape)), axis, 0, 0, t...  75.1 us
    psum x4, blocking collectives, over_axes(): return functools.reduce(lax.psum, axes, x)  54.8 us
    all_to_all x1, blocking collectives, sum_at_owner(): lax.all_to_all(blocks, axis, split_axis=0, concat_axis=0, tiled=True)  32.1 us
    all_to_all x2, starting transfers between devices, copy_for_each(): lax.all_to_all(jnp.broadcast_to(x[None], (size, *x.shape)), axis, 0, 0, t...  12.1 us
    all_to_all x2, waiting for transfers between devices, copy_for_each(): lax.all_to_all(jnp.broadcast_to(x[None], (size, *x.shape)), axis, 0, 0, t...  10.8 us
    dot_general x3, matrix products, project_rows(): lax.dot_general(normed, embed_table, (((1,), (1,)), ((), ())), preferred_...  8.1 us
    reshape x2, local copies, waits for them, and re-layouts, in_blocks(): x.reshape(*lengths[:dim], size, lengths[dim] // size, *lengths[dim + 1:])  6.51 us
    reshape x3, local copies, waits for them, and re-layouts, joined_along(): blocks.reshape(*lengths[:dim], lengths[dim] * lengths[dim + 1], *lengths[...  6.34 us
  transfers between devices with their start and end apart: 2, of which 2 were waited for; matrix products, arithmetic and copies ran while one was open for 4% of the time, Pallas kernels for 0%

commit v1 on v0

v1 whole, which is shorter than its diff:
```python
import math

import jax
import jax.numpy as jnp
from jax import lax
from jax.sharding import Mesh
from jax.sharding import PartitionSpec as P

D = 4608
STEPS = 3
XY = ("dp_0", "dp_1")
DP = ("dp_0", "dp_1", "dp_2")
DP_VOCAB = ("dp_0", "dp_1", "dp_2", "vocab")
SLOTS = 8

epsilon_value = 1e-06
softcap_value = 30.0


def exchange(x, axis):
    return lax.all_to_all(x, axis, split_axis=0, concat_axis=0, tiled=True)


def to_each(x, axis):
    return exchange(jnp.broadcast_to(x[None], (lax.axis_size(axis), *x.shape)), axis)


def other_core(x):
    return lax.ppermute(x, "dp_2", [(0, 1), (1, 0)])


def in_three(x):
    high = lax.reduce_precision(x, 8, 7)
    middle = lax.reduce_precision(x - high, 8, 7)
    return jnp.concatenate([high, middle, x - high - middle], axis=-1).astype(jnp.bfloat16)


def on_device(hidden, norm_gain, embed_table, tokens):
    own_rows = hidden.shape[0]
    shard_rows = embed_table.shape[0]
    n_xy = lax.axis_size(XY)
    core = lax.axis_index("dp_2")
    shard_start = (
        lax.axis_index(DP) * lax.axis_size("vocab") + lax.axis_index("vocab")
    ) * shard_rows
    scale_factor = math.sqrt(D)
    used = STEPS * own_rows

    ids = jnp.transpose(tokens.reshape(n_xy, 2, own_rows, STEPS), (1, 0, 3, 2))
    ids = ids.reshape(2, n_xy, used) - shard_start
    ids = jnp.pad(ids, ((0, 0), (0, 0), (0, SLOTS - used)), constant_values=-1)
    mine = jnp.where(core == 0, ids[0], ids[1]).reshape(n_xy * SLOTS)
    theirs = jnp.where(core == 0, ids[1], ids[0]).reshape(n_xy * SLOTS)
    columns = lax.broadcasted_iota(jnp.int32, (1, shard_rows), 1)
    match_mine = mine[:, None] == columns
    match_theirs = theirs[:, None] == columns

    def rows_of(match):
        return jnp.dot(
            match.astype(jnp.bfloat16), embed_table, preferred_element_type=jnp.float32
        ).astype(jnp.bfloat16)

    arriving = other_core(rows_of(match_theirs))
    found = (rows_of(match_mine) + arriving).reshape(n_xy, SLOTS, D)
    held = exchange(found, XY).astype(jnp.float32).sum(axis=0).astype(jnp.bfloat16)
    first = to_each(held[: 2 * own_rows], "vocab").astype(jnp.float32).sum(axis=0)

    currents = [hidden]
    for step in range(2):
        looked = first[step * own_rows : (step + 1) * own_rows]
        currents.append(currents[-1] + scale_factor * looked)
    states = jnp.concatenate(currents, axis=0)
    square_mean = jnp.mean(states * states, axis=-1, keepdims=True)
    normed = (states * lax.rsqrt(square_mean + epsilon_value) * norm_gain).astype(jnp.bfloat16)
    normed = jnp.pad(normed, ((0, SLOTS - used), (0, 0)))
    of_mine = to_each(normed, XY).reshape(n_xy * SLOTS, D)
    of_theirs = other_core(of_mine)

    def totals(rows, match):
        logits = lax.dot_general(
            rows, embed_table, (((1,), (1,)), ((), ())), preferred_element_type=jnp.float32
        )
        capped = softcap_value * jnp.tanh(logits / softcap_value)
        exp_total = jnp.sum(jnp.exp(capped), axis=-1)
        target = jnp.sum(jnp.where(match, capped, 0.0), axis=-1)
        return jnp.concatenate(
            [exp_total.reshape(n_xy, SLOTS), target.reshape(n_xy, SLOTS)], axis=1
        )

    for_mine = totals(of_mine, match_mine)
    for_theirs = totals(of_theirs, match_theirs)
    for_0 = jnp.where(core == 0, for_mine, for_theirs)
    for_1 = jnp.where(core == 0, for_theirs, for_mine)
    parts = jnp.stack([for_0, for_1], axis=1).reshape(2 * n_xy, 1, 2 * SLOTS)
    parts = jnp.pad(parts, ((0, 0), (0, 0), (0, 128 - 2 * SLOTS)))
    part = exchange(parts, DP).sum(axis=0)[:, : 2 * SLOTS]
    part = jnp.pad(in_three(part), ((0, own_rows - 1), (0, 128 - 6 * SLOTS)))
    last = jnp.concatenate([held[2 * own_rows : used], part], axis=1)
    last = to_each(last, "vocab").astype(jnp.float32).sum(axis=0)
    whole = last[0, D : D + 6 * SLOTS].reshape(3, 2, SLOTS).sum(axis=0)
    log_probs = whole[1, :used] - jnp.log(whole[0, :used])
    final_hidden = currents[2] + scale_factor * last[:, :D]
    return (jnp.transpose(log_probs.reshape(STEPS, own_rows)), final_hidden)


def solution(mesh):
    finer = Mesh(
        mesh.devices.reshape(4, 4, 2, mesh.shape["vocab"]), ("dp_0", "dp_1", "dp_2", "vocab")
    )
    in_specs = (P(DP, None), P(), P(DP_VOCAB, None), P())
    out_specs = (P(DP, None), P(DP, None))
    return jax.shard_map(
        on_device, mesh=finer, in_specs=in_specs, out_specs=out_specs, check_vma=False
    )
```

time: 224 us -> 164 us (0.73)
  the two profiles are of different devices: /device:TPU:2 before, /device:TPU:64 now
where the time goes in v1:
time: 164 us
  blocking collectives  119 us (73%)
  matrix products  10.1 us (6%)
  local copies, waits for them, and re-layouts  10 us (6%)
  waiting for transfers between devices  8.86 us (5%)
  starting transfers between devices  7.8 us (5%)
  other arithmetic  7.13 us (4%)
    all_to_all x4, blocking collectives, exchange(): return lax.all_to_all(x, axis, split_axis=0, concat_axis=0, tiled=True)  119 us
    dot_general x2, matrix products, totals(): lax.dot_general(rows, embed_table, (((1,), (1,)), ((), ())), preferred_el...  6.2 us
    all_to_all x1, waiting for transfers between devices, exchange(): return lax.all_to_all(x, axis, split_axis=0, concat_axis=0, tiled=True)  5.86 us
    all_to_all x1, starting transfers between devices, exchange(): return lax.all_to_all(x, axis, split_axis=0, concat_axis=0, tiled=True)  3.98 us
    dot_general x2, matrix products, rows_of(): jnp.dot(match.astype(jnp.bfloat16), embed_table, preferred_element_type=j...  3.92 us
    ppermute x2, starting transfers between devices, other_core(): return lax.ppermute(x, 'dp_2', [(0, 1), (1, 0)])  3.82 us
    concatenate x4, local copies, waits for them, and re-layouts, totals(): jnp.concatenate([exp_total.reshape(n_xy, SLOTS), target.reshape(n_xy, SLO...  3.4 us
  transfers between devices with their start and end apart: 3, of which 2 were waited for; matrix products, arithmetic and copies ran while one was open for 3% of the time, Pallas kernels for 0%

profile of v1, /device:TPU:64, one launch (start us, length us, event | category | flops | bytes accessed | tf_op | source)
XLA Modules:
  0.0 163.6 jit_solution(149883078490290744)
XLA Ops:
  0.6 0.0 copy-start
  0.7 0.8 broadcast_subtract_fusion
  1.5 0.8 sub.31
  2.2 0.9 copy.33
  3.2 0.1 copy.35
  3.2 0.1 select_n.63
  3.3 0.0 copy-done
  3.3 0.0 copy-start.5
  3.4 1.8 %convolution_convert_fusion = bf16[128,4608]{1,0:T(8,128)(2,1)} fusion(bf16[384,4608]{1,0:T(8,128)(2,1)S(1)} %copy-done, s32[128]{0:T(128)S(1)} %select_n.63), kind=kOutput, calls=%fused_computation | convolution fusion | flops 453623808 | bytes 4719104 | tf_op jit(solution)/shard_map/dot_general | solution.py:59
  5.2 0.0 copy-done.5
  5.2 1.9 %collective-permute-start = (bf16[128,4608]{1,0:T(8,128)(2,1)}, bf16[128,4608]{1,0:T(8,128)(2,1)}, u32[]{:S(2)}, u32[]{:S(2)}) collective-permute-start(bf16[128,4608]{1,0:T(8,128)(2,1)} %convolution_convert_fusion), channel_id=1, source_target_pairs={{0,16},{16,0},{1,17},{17,1},{2,18},{18,2},{3,19},{19,3},{4,20},{20... | collective-permute-start | bytes 3538952 | tf_op jit(solution)/shard_map/ppermute | solution.py:29
  7.1 0.1 copy.34
  7.2 0.1 select_n.61
  7.3 3.0 %collective-permute-done = bf16[128,4608]{1,0:T(8,128)(2,1)} collective-permute-done((bf16[128,4608]{1,0:T(8,128)(2,1)}, bf16[128,4608]{1,0:T(8,128)(2,1)}, u32[]{:S(2)}, u32[]{:S(2)}) %collective-permute-start) | collective-permute-done | bytes 1179680 | tf_op jit(solution)/shard_map/ppermute | solution.py:29
  10.3 2.1 %fusion.1 = bf16[16,8,4608]{2,1,0:T(8,128)(2,1)S(1)} fusion(bf16[128,4608]{1,0:T(8,128)(2,1)} %collective-permute-done, bf16[384,4608]{1,0:T(8,128)(2,1)S(1)} %copy-done, s32[128]{0:T(128)S(1)} %select_n.61), kind=kOutput, calls=%fused_computation.3 | convolution fusion | flops 454213632 | bytes 5898752 | tf_op jit(solution)/shard_map/dot_general | solution.py:59
  12.4 25.6 %all_to_all.25 = bf16[16,8,4608]{2,1,0:T(8,128)(2,1)} all-to-all(bf16[16,8,4608]{2,1,0:T(8,128)(2,1)S(1)} %fusion.1), channel_id=1, replica_groups=mesh['dp_0'=4,'dp_1'=4,'dp_2'=2,'vocab'=16] {'dp_0','dp_1'}, dimensions={0} | all-to-all | bytes 2359296 | tf_op jit(solution)/shard_map/all_to_all | solution.py:21
  38.0 2.1 %reduce_sum.95 = bf16[8,4608]{1,0:T(8,128)(2,1)} reduce(bf16[16,8,4608]{2,1,0:T(8,128)(2,1)} %all_to_all.25, bf16[]{:T(256)} %constant.42.clone.1), dimensions={0}, to_apply=%region_0.1 | reduce | flops 552960 | bytes 1253378 | tf_op jit(solution)/shard_map/reduce_sum | solution.py:65
  40.0 0.9 slice.47
  40.9 0.0 copy-start.3
  40.9 0.2 broadcast_in_dim.10
  41.1 0.0 copy-start.4
  41.1 46.8 %all_to_all.26 = bf16[16,4,4608]{2,1,0:T(4,128)(2,1)S(1)} all-to-all(bf16[16,4,4608]{2,1,0:T(4,128)(2,1)S(1)} %broadcast_in_dim.10), channel_id=1, replica_groups=mesh['dp_0'=4,'dp_1'=4,'dp_2'=2,'vocab'=16] {'vocab'}, dimensions={0} | all-to-all | bytes 1179648 | tf_op jit(solution)/shard_map/all_to_all | solution.py:21
  87.9 0.2 convert_reduce_fusion
  88.1 0.0 copy-done.3
  88.2 0.1 fusion.9
  88.2 0.0 copy-start.1
  88.2 0.2 multiply_reduce_fusion
  88.4 0.0 copy-done.4
  88.4 0.1 multiply_convert_fusion
  88.5 0.3 copy-done.1
  88.8 0.1 broadcast_in_dim.12
  88.9 20.0 %all_to_all.27 = bf16[16,8,4608]{2,1,0:T(8,128)(2,1)} all-to-all(bf16[16,8,4608]{2,1,0:T(8,128)(2,1)S(1)} %broadcast_in_dim.12), channel_id=1, replica_groups=mesh['dp_0'=4,'dp_1'=4,'dp_2'=2,'vocab'=16] {'dp_0','dp_1'}, dimensions={0} | all-to-all | bytes 2359296 | tf_op jit(solution)/shard_map/all_to_all | solution.py:21
  108.9 1.9 %collective-permute-start.1 = (bf16[128,4608]{1,0:T(8,128)(2,1)}, bf16[128,4608]{1,0:T(8,128)(2,1)}, u32[]{:S(2)}, u32[]{:S(2)}) collective-permute-start(bf16[128,4608]{1,0:T(8,128)(2,1)} %bitcast.3), channel_id=1, source_target_pairs={{0,16},{16,0},{1,17},{17,1},{2,18},{18,2},{3,19},{19,3},{4,20},{20... | collective-permute-start | bytes 3538952 | tf_op jit(solution)/shard_map/ppermute | solution.py:29
  110.9 3.1 %exponential_reduce_fusion.1 = (f32[128]{0:T(128)S(1)}, f32[128]{0:T(128)}) fusion(s32[128]{0:T(128)S(1)} %select_n.61, bf16[384,4608]{1,0:T(8,128)(2,1)S(1)} %copy-done, bf16[16,8,4608]{2,1,0:T(8,128)(2,1)} %all_to_all.27), kind=kOutput, calls=%fused_computation.15 | convolution fusion | flops 453279488 | bytes 4720128 | tf_op jit(solution)/shard_map/dot_general | solution.py:80
  113.9 0.1 concatenate.61
  114.0 0.7 concatenate.62
  114.7 0.0 collective-permute-done.1
  114.7 3.1 %exponential_reduce_fusion = (f32[128]{0:T(128)}, f32[128]{0:T(128)}) fusion(s32[128]{0:T(128)} %copy-done.5, bf16[128,4608]{1,0:T(8,128)(2,1)} %collective-permute-done.1, bf16[384,4608]{1,0:T(8,128)(2,1)S(1)} %copy-done), kind=kOutput, calls=%fused_computation.13 | convolution fusion | flops 453279488 | bytes 4720128 | tf_op jit(solution)/shard_map/dot_general | solution.py:80
  117.8 1.3 concatenate.64
  119.1 1.3 concatenate.65
  120.5 0.8 broadcast_select_fusion.3
  121.3 0.6 pad.18
  121.9 4.0 %all-to-all-start.3 = ((f32[32,1,128]{2,1,0:T(1,128)}), f32[32,1,128]{2,1,0:T(1,128)S(1)}, u32[]{:S(2)}, u32[]{:S(2)}) async-start(f32[32,1,128]{2,1,0:T(1,128)} %bitcast.21), calls=%async_computation.3 | async-start | bytes 32768 | tf_op jit(solution)/shard_map/all_to_all | solution.py:21
  125.9 1.5 slice.46
  127.4 5.9 %all-to-all-done.3 = f32[32,1,128]{2,1,0:T(1,128)S(1)} async-done(((f32[32,1,128]{2,1,0:T(1,128)}), f32[32,1,128]{2,1,0:T(1,128)S(1)}, u32[]{:S(2)}, u32[]{:S(2)}) %all-to-all-start.3) | async-done | bytes 16416 | tf_op jit(solution)/shard_map/all_to_all | solution.py:21
  133.2 0.6 reduce_sum.102
  133.8 0.0 copy-start.2
  133.8 0.7 reduce-precision_convert_fusion.1
  134.5 0.1 fusion.19
  134.5 0.7 pad_maximum_fusion.1
  135.3 0.2 broadcast_in_dim.14
  135.5 26.5 %all_to_all.28 = bf16[16,2,4736]{2,1,0:T(2,128)(2,1)S(1)} all-to-all(bf16[16,2,4736]{2,1,0:T(2,128)(2,1)S(1)} %broadcast_in_dim.14), channel_id=1, replica_groups=mesh['dp_0'=4,'dp_1'=4,'dp_2'=2,'vocab'=16] {'vocab'}, dimensions={0} | all-to-all | bytes 606208 | tf_op jit(solution)/shard_map/all_to_all | solution.py:21
  161.9 0.1 convert_reduce_fusion.1
  162.1 0.0 copy-done.2
  162.1 0.6 fusion.8
  162.7 0.1 reshape_squeeze.3
  162.9 0.1 sub.37
  162.9 0.7 copy.40
  (8 shorter events, 0.1 us)
Async XLA Ops:
  0.6 2.7 %copy-start = (bf16[384,4608]{1,0:T(8,128)(2,1)S(1)}, bf16[384,4608]{1,0:T(8,128)(2,1)}, u32[]{:S(2)}) copy-start(bf16[384,4608]{1,0:T(8,128)(2,1)} %param.6) | copy-start | bytes 10616836
  3.3 1.8 %copy-start.5 = (s32[128]{0:T(128)}, s32[128]{0:T(128)S(1)}, u32[]{:S(2)}) copy-start(s32[128]{0:T(128)S(1)} %select_n.63) | copy-start | bytes 1540
  5.2 5.1 %collective-permute-start = (bf16[128,4608]{1,0:T(8,128)(2,1)}, bf16[128,4608]{1,0:T(8,128)(2,1)}, u32[]{:S(2)}, u32[]{:S(2)}) collective-permute-start(bf16[128,4608]{1,0:T(8,128)(2,1)} %convolution_convert_fusion), channel_id=1, source_target_pairs={{0,16},{16,0},{1,17},{17,1},{2,18},{18,2},{3,19},{19,3},{4,20},{20... | collective-permute-start | bytes 3538952 | tf_op jit(solution)/shard_map/ppermute | solution.py:29
  40.9 47.2 %copy-start.3 = (f32[2,4608]{1,0:T(2,128)S(1)}, f32[2,4608]{1,0:T(2,128)}, u32[]{:S(2)}) copy-start(f32[2,4608]{1,0:T(2,128)} %param.4) | copy-start | bytes 110596
  41.1 47.3 %copy-start.4 = (f32[4608]{0:T(1024)S(1)}, f32[4608]{0:T(1024)}, u32[]{:S(2)}) copy-start(f32[4608]{0:T(1024)} %param.5) | copy-start | bytes 55300
  88.2 0.6 copy-start.1
  108.9 5.7 %collective-permute-start.1 = (bf16[128,4608]{1,0:T(8,128)(2,1)}, bf16[128,4608]{1,0:T(8,128)(2,1)}, u32[]{:S(2)}, u32[]{:S(2)}) collective-permute-start(bf16[128,4608]{1,0:T(8,128)(2,1)} %bitcast.3), channel_id=1, source_target_pairs={{0,16},{16,0},{1,17},{17,1},{2,18},{18,2},{3,19},{19,3},{4,20},{20... | collective-permute-start | bytes 3538952 | tf_op jit(solution)/shard_map/ppermute | solution.py:29
  121.9 11.3 %all-to-all-start.3 = ((f32[32,1,128]{2,1,0:T(1,128)}), f32[32,1,128]{2,1,0:T(1,128)S(1)}, u32[]{:S(2)}, u32[]{:S(2)}) async-start(f32[32,1,128]{2,1,0:T(1,128)} %bitcast.21), calls=%async_computation.3 | async-start | bytes 32768 | tf_op jit(solution)/shard_map/all_to_all | solution.py:21
  133.8 28.3 %copy-start.2 = (f32[2,4608]{1,0:T(2,128)S(1)}, f32[2,4608]{1,0:T(2,128)}, u32[]{:S(2)}) copy-start(f32[2,4608]{1,0:T(2,128)} %copy-done.1) | copy-start | bytes 110596

commit v2 on v1

--- a/solution.py
+++ b/solution.py
@@ -29,12 +29,6 @@
     return lax.ppermute(x, "dp_2", [(0, 1), (1, 0)])
 
 
-def in_three(x):
-    high = lax.reduce_precision(x, 8, 7)
-    middle = lax.reduce_precision(x - high, 8, 7)
-    return jnp.concatenate([high, middle, x - high - middle], axis=-1).astype(jnp.bfloat16)
-
-
 def on_device(hidden, norm_gain, embed_table, tokens):
     own_rows = hidden.shape[0]
     shard_rows = embed_table.shape[0]
@@ -63,13 +57,13 @@
     arriving = other_core(rows_of(match_theirs))
     found = (rows_of(match_mine) + arriving).reshape(n_xy, SLOTS, D)
     held = exchange(found, XY).astype(jnp.float32).sum(axis=0).astype(jnp.bfloat16)
-    first = to_each(held[: 2 * own_rows], "vocab").astype(jnp.float32).sum(axis=0)
+    looked = lax.all_gather(held[:used].reshape(STEPS, own_rows, D), "vocab")
+    looked = looked.astype(jnp.float32).sum(axis=0)
 
     currents = [hidden]
-    for step in range(2):
-        looked = first[step * own_rows : (step + 1) * own_rows]
-        currents.append(currents[-1] + scale_factor * looked)
-    states = jnp.concatenate(currents, axis=0)
+    for step in range(STEPS):
+        currents.append(currents[-1] + scale_factor * looked[step])
+    states = jnp.concatenate(currents[:STEPS], axis=0)
     square_mean = jnp.mean(states * states, axis=-1, keepdims=True)
     normed = (states * lax.rsqrt(square_mean + epsilon_value) * norm_gain).astype(jnp.bfloat16)
     normed = jnp.pad(normed, ((0, SLOTS - used), (0, 0)))
@@ -83,24 +77,19 @@
         capped = softcap_value * jnp.tanh(logits / softcap_value)
         exp_total = jnp.sum(jnp.exp(capped), axis=-1)
         target = jnp.sum(jnp.where(match, capped, 0.0), axis=-1)
-        return jnp.concatenate(
-            [exp_total.reshape(n_xy, SLOTS), target.reshape(n_xy, SLOTS)], axis=1
-        )
+        return jnp.stack([exp_total, target])
 
     for_mine = totals(of_mine, match_mine)
     for_theirs = totals(of_theirs, match_theirs)
-    for_0 = jnp.where(core == 0, for_mine, for_theirs)
-    for_1 = jnp.where(core == 0, for_theirs, for_mine)
-    parts = jnp.stack([for_0, for_1], axis=1).reshape(2 * n_xy, 1, 2 * SLOTS)
-    parts = jnp.pad(parts, ((0, 0), (0, 0), (0, 128 - 2 * SLOTS)))
-    part = exchange(parts, DP).sum(axis=0)[:, : 2 * SLOTS]
-    part = jnp.pad(in_three(part), ((0, own_rows - 1), (0, 128 - 6 * SLOTS)))
-    last = jnp.concatenate([held[2 * own_rows : used], part], axis=1)
-    last = to_each(last, "vocab").astype(jnp.float32).sum(axis=0)
-    whole = last[0, D : D + 6 * SLOTS].reshape(3, 2, SLOTS).sum(axis=0)
-    log_probs = whole[1, :used] - jnp.log(whole[0, :used])
-    final_hidden = currents[2] + scale_factor * last[:, :D]
-    return (jnp.transpose(log_probs.reshape(STEPS, own_rows)), final_hidden)
+    halves = jnp.where(
+        core == 0, jnp.stack([for_mine, for_theirs]), jnp.stack([for_theirs, for_mine])
+    )
+    parts = jnp.broadcast_to(halves[None], (n_xy, *halves.shape))
+    part = exchange(parts.reshape(2 * n_xy, *halves.shape[1:]), DP).sum(axis=0)
+    whole = to_each(part, "vocab").sum(axis=0)
+    log_probs = whole[1] - jnp.log(whole[0])
+    log_probs = lax.dynamic_slice_in_dim(log_probs, lax.axis_index(XY) * SLOTS, used)
+    return (jnp.transpose(log_probs.reshape(STEPS, own_rows)), currents[STEPS])
 
 
 def solution(mesh):

time: 164 us -> 142 us (0.87)
  the two profiles are of different devices: /device:TPU:64 before, /device:TPU:1 now
where the time goes in v2:
time: 142 us; the launch traced here: 141 us
  blocking collectives  80.3 us (57%)
  starting transfers between devices  26.7 us (19%)
  waiting for transfers between devices  15.2 us (11%)
  other arithmetic  6.78 us (5%)
  matrix products  6.5 us (5%)
  local copies, waits for them, and re-layouts  5.08 us (4%)
    all_to_all x3, blocking collectives, exchange(): return lax.all_to_all(x, axis, split_axis=0, concat_axis=0, tiled=True)  47.7 us
    all_gather x1, blocking collectives, on_device(): looked = lax.all_gather(held[:used].reshape(STEPS, own_rows, D), 'vocab')  32.5 us
    ppermute x2, starting transfers between devices, other_core(): return lax.ppermute(x, 'dp_2', [(0, 1), (1, 0)])  20.4 us
    all_to_all x1, waiting for transfers between devices, exchange(): return lax.all_to_all(x, axis, split_axis=0, concat_axis=0, tiled=True)  11.4 us
    all_to_all x1, starting transfers between devices, exchange(): return lax.all_to_all(x, axis, split_axis=0, concat_axis=0, tiled=True)  6.31 us
    dot_general x2, matrix products, rows_of(): jnp.dot(match.astype(jnp.bfloat16), embed_table, preferred_element_type=j...  3.93 us
    ppermute x2, waiting for transfers between devices, other_core(): return lax.ppermute(x, 'dp_2', [(0, 1), (1, 0)])  3.79 us
  transfers between devices with their start and end apart: 3, of which 3 were waited for; matrix products, arithmetic and copies ran while one was open for 1% of the time, Pallas kernels for 0%

profile of v2, /device:TPU:1, one launch (start us, length us, event | category | flops | bytes accessed | tf_op | source)
XLA Modules:
  0.0 141.3 jit_solution(1392646307839369335)
XLA Ops:
  0.6 0.0 copy-start
  0.7 0.8 broadcast_subtract_fusion
  1.5 0.8 sub.21
  2.2 0.9 copy.21
  3.2 0.1 copy.23
  3.2 0.1 select_n.53
  3.3 0.0 copy-done
  3.3 1.8 %convolution_convert_fusion = bf16[128,4608]{1,0:T(8,128)(2,1)} fusion(bf16[384,4608]{1,0:T(8,128)(2,1)S(1)} %copy-done, s32[128]{0:T(128)S(1)} %select_n.53), kind=kOutput, calls=%fused_computation | convolution fusion | flops 453623808 | bytes 4719104 | tf_op jit(solution)/shard_map/dot_general | solution.py:53
  5.2 8.8 %collective-permute-start = (bf16[128,4608]{1,0:T(8,128)(2,1)}, bf16[128,4608]{1,0:T(8,128)(2,1)}, u32[]{:S(2)}, u32[]{:S(2)}) collective-permute-start(bf16[128,4608]{1,0:T(8,128)(2,1)} %convolution_convert_fusion), channel_id=1, source_target_pairs={{0,16},{16,0},{1,17},{17,1},{2,18},{18,2},{3,19},{19,3},{4,20},{20... | collective-permute-start | bytes 3538952 | tf_op jit(solution)/shard_map/ppermute | solution.py:29
  14.0 0.1 copy.22
  14.0 0.1 select_n.51
  14.1 2.6 %collective-permute-done = bf16[128,4608]{1,0:T(8,128)(2,1)} collective-permute-done((bf16[128,4608]{1,0:T(8,128)(2,1)}, bf16[128,4608]{1,0:T(8,128)(2,1)}, u32[]{:S(2)}, u32[]{:S(2)}) %collective-permute-start) | collective-permute-done | bytes 1179680 | tf_op jit(solution)/shard_map/ppermute | solution.py:29
  16.8 2.1 %fusion.1 = bf16[16,8,4608]{2,1,0:T(8,128)(2,1)S(1)} fusion(bf16[128,4608]{1,0:T(8,128)(2,1)} %collective-permute-done, bf16[384,4608]{1,0:T(8,128)(2,1)S(1)} %copy-done, s32[128]{0:T(128)S(1)} %select_n.51), kind=kOutput, calls=%fused_computation.3 | convolution fusion | flops 454213632 | bytes 5898752 | tf_op jit(solution)/shard_map/dot_general | solution.py:53
  18.9 21.2 %all_to_all.20 = bf16[16,8,4608]{2,1,0:T(8,128)(2,1)} all-to-all(bf16[16,8,4608]{2,1,0:T(8,128)(2,1)S(1)} %fusion.1), channel_id=1, replica_groups=mesh['dp_0'=4,'dp_1'=4,'dp_2'=2,'vocab'=16] {'dp_0','dp_1'}, dimensions={0} | all-to-all | bytes 2359296 | tf_op jit(solution)/shard_map/all_to_all | solution.py:21
  40.0 2.1 %reduce_sum.84 = bf16[8,4608]{1,0:T(8,128)(2,1)} reduce(bf16[16,8,4608]{2,1,0:T(8,128)(2,1)} %all_to_all.20, bf16[]{:T(256)} %constant.44.clone.1), dimensions={0}, to_apply=%region_0.1 | reduce | flops 552960 | bytes 1253378 | tf_op jit(solution)/shard_map/reduce_sum | solution.py:59
  42.1 1.6 %all_gather_reshape.3 = bf16[1,3,2,4608]{3,2,1,0:T(2,128)(2,1)} reshape(bf16[6,4608]{1,0:T(8,128)(2,1)} %bitcast.42) | data formatting | bytes 110592 | tf_op jit(solution)/shard_map/all_gather;reshape | solution.py:60
  43.7 0.0 copy-start.1
  43.7 0.0 copy-start.2
  43.7 32.5 %all_gather.3 = bf16[16,3,2,4608]{3,2,1,0:T(2,128)(2,1)S(1)} all-gather(bf16[1,3,2,4608]{3,2,1,0:T(2,128)(2,1)} %all_gather_reshape.3), channel_id=1, replica_groups=mesh['dp_0'=4,'dp_1'=4,'dp_2'=2,'vocab'=16] {'vocab'}, dimensions={0}, use_global_device_ids=true | all-gather | bytes 940032 | tf_op jit(solution)/shard_map/all_gather | solution.py:60
  76.2 0.7 convert_reduce_fusion
  77.0 0.0 copy-done.1
  77.0 0.7 fusion.9
  77.6 0.2 multiply_reduce_fusion
  77.8 0.0 copy-done.2
  77.8 0.1 multiply_convert_fusion
  78.0 0.1 broadcast_in_dim.11
  78.0 15.3 %all_to_all.21 = bf16[16,8,4608]{2,1,0:T(8,128)(2,1)S(1)} all-to-all(bf16[16,8,4608]{2,1,0:T(8,128)(2,1)S(1)} %broadcast_in_dim.11), channel_id=1, replica_groups=mesh['dp_0'=4,'dp_1'=4,'dp_2'=2,'vocab'=16] {'dp_0','dp_1'}, dimensions={0} | all-to-all | bytes 2359296 | tf_op jit(solution)/shard_map/all_to_all | solution.py:21
  93.4 11.6 %collective-permute-start.1 = (bf16[128,4608]{1,0:T(8,128)(2,1)S(1)}, bf16[128,4608]{1,0:T(8,128)(2,1)S(1)}, u32[]{:S(2)}, u32[]{:S(2)}) collective-permute-start(bf16[128,4608]{1,0:T(8,128)(2,1)S(1)} %bitcast.41), channel_id=1, source_target_pairs={{0,16},{16,0},{1,17},{17,1},{2,18},{18,2},{3,19},{19,3},{4,20},{20... | collective-permute-start | bytes 3538952 | tf_op jit(solution)/shard_map/ppermute | solution.py:29
  105.0 1.3 exponential_reduce_fusion.1
  106.3 1.2 collective-permute-done.1
  107.5 1.3 exponential_reduce_fusion
  108.8 11.2 %all_to_all.22 = f32[32,2,128]{2,1,0:T(2,128)} all-to-all(f32[32,2,128]{2,1,0:T(2,128)S(1)} %bitcast.44), channel_id=1, replica_groups=mesh['dp_0'=4,'dp_1'=4,'dp_2'=2,'vocab'=16] {'dp_0','dp_1','dp_2'}, dimensions={0} | all-to-all | bytes 65536 | tf_op jit(solution)/shard_map/all_to_all | solution.py:21
  120.0 0.8 reduce_sum.91
  120.8 0.6 broadcast_in_dim.14
  121.4 6.3 %all-to-all-start.3 = ((f32[16,2,128]{2,1,0:T(2,128)}), f32[16,2,128]{2,1,0:T(2,128)S(1)}, u32[]{:S(2)}, u32[]{:S(2)}) async-start(f32[16,2,128]{2,1,0:T(2,128)} %broadcast_in_dim.14), calls=%async_computation.3 | async-start | bytes 32768 | tf_op jit(solution)/shard_map/all_to_all | solution.py:21
  127.7 11.4 %all-to-all-done.3 = f32[16,2,128]{2,1,0:T(2,128)S(1)} async-done(((f32[16,2,128]{2,1,0:T(2,128)}), f32[16,2,128]{2,1,0:T(2,128)S(1)}, u32[]{:S(2)}, u32[]{:S(2)}) %all-to-all-start.3) | async-done | bytes 16416 | tf_op jit(solution)/shard_map/all_to_all | solution.py:21
  139.1 0.6 reduce_sum.92
  139.7 0.8 log_subtract_fusion
  140.5 0.1 dynamic-slice_reduce_fusion
  140.5 0.1 reshape.101
  140.6 0.7 copy.26
  (6 shorter events, 0.1 us)
Async XLA Ops:
  0.6 2.7 %copy-start = (bf16[384,4608]{1,0:T(8,128)(2,1)S(1)}, bf16[384,4608]{1,0:T(8,128)(2,1)}, u32[]{:S(2)}) copy-start(bf16[384,4608]{1,0:T(8,128)(2,1)} %param.6) | copy-start | bytes 10616836
  5.2 11.6 %collective-permute-start = (bf16[128,4608]{1,0:T(8,128)(2,1)}, bf16[128,4608]{1,0:T(8,128)(2,1)}, u32[]{:S(2)}, u32[]{:S(2)}) collective-permute-start(bf16[128,4608]{1,0:T(8,128)(2,1)} %convolution_convert_fusion), channel_id=1, source_target_pairs={{0,16},{16,0},{1,17},{17,1},{2,18},{18,2},{3,19},{19,3},{4,20},{20... | collective-permute-start | bytes 3538952 | tf_op jit(solution)/shard_map/ppermute | solution.py:29
  43.7 33.3 %copy-start.1 = (f32[2,4608]{1,0:T(2,128)S(1)}, f32[2,4608]{1,0:T(2,128)}, u32[]{:S(2)}) copy-start(f32[2,4608]{1,0:T(2,128)} %param.4) | copy-start | bytes 110596
  43.7 34.2 %copy-start.2 = (f32[4608]{0:T(1024)S(1)}, f32[4608]{0:T(1024)}, u32[]{:S(2)}) copy-start(f32[4608]{0:T(1024)} %param.5) | copy-start | bytes 55300
  93.4 14.1 %collective-permute-start.1 = (bf16[128,4608]{1,0:T(8,128)(2,1)S(1)}, bf16[128,4608]{1,0:T(8,128)(2,1)S(1)}, u32[]{:S(2)}, u32[]{:S(2)}) collective-permute-start(bf16[128,4608]{1,0:T(8,128)(2,1)S(1)} %bitcast.41), channel_id=1, source_target_pairs={{0,16},{16,0},{1,17},{17,1},{2,18},{18,2},{3,19},{19,3},{4,20},{20... | collective-permute-start | bytes 3538952 | tf_op jit(solution)/shard_map/ppermute | solution.py:29
  121.4 17.7 %all-to-all-start.3 = ((f32[16,2,128]{2,1,0:T(2,128)}), f32[16,2,128]{2,1,0:T(2,128)S(1)}, u32[]{:S(2)}, u32[]{:S(2)}) async-start(f32[16,2,128]{2,1,0:T(2,128)} %broadcast_in_dim.14), calls=%async_computation.3 | async-start | bytes 32768 | tf_op jit(solution)/shard_map/all_to_all | solution.py:21

commit v3 on v2

v3 whole, which is shorter than its diff:
```python
import functools
import math

import jax
import jax.numpy as jnp
from jax import lax
from jax.experimental import pallas as pl
from jax.experimental.pallas import tpu as pltpu
from jax.sharding import Mesh
from jax.sharding import PartitionSpec as P

D = 4608
STEPS = 3
XY = ("dp_0", "dp_1")
DP = ("dp_0", "dp_1", "dp_2")
DP_VOCAB = ("dp_0", "dp_1", "dp_2", "vocab")
ROOM = 2
SLOTS = 8

epsilon_value = 1e-06
softcap_value = 30.0


def exchange(x, axis):
    return lax.all_to_all(x, axis, split_axis=0, concat_axis=0, tiled=True)


def to_each(x, axis):
    return exchange(jnp.broadcast_to(x[None], (lax.axis_size(axis), *x.shape)), axis)


def other_core(x):
    return lax.ppermute(x, "dp_2", [(0, 1), (1, 0)])


def picked(block, index):
    rows = lax.broadcasted_iota(jnp.int32, block.shape, 0)
    return jnp.sum(jnp.where(rows == index, block.astype(jnp.float32), 0.0), axis=0, keepdims=True)


def placed(row, index, count):
    rows = lax.broadcasted_iota(jnp.int32, (count, row.shape[1]), 0)
    return jnp.where(rows == index, row, 0.0)


def lookup_kernel(turn, tokens, table, rows, ids, held, found, sem):
    steps, summaries = tokens.shape
    shard_rows = table.shape[0]
    own_rows = summaries // rows.shape[0]
    start = (
        lax.axis_index(DP) * lax.axis_size("vocab") + lax.axis_index("vocab")
    ) * shard_rows
    core = lax.axis_index("dp_2")
    copy = pltpu.make_async_copy(table, held, sem)
    copy.start()
    rows[...] = jnp.zeros_like(rows)
    half_of = lax.broadcasted_iota(jnp.int32, ids.shape, 0)
    lane_of = lax.broadcasted_iota(jnp.int32, ids.shape, 1)

    def scan(group, state):
        n, all_ids = state
        count = jnp.int32(0)
        half = jnp.where(group % 2 == core, 0, 1)
        for step in range(steps):
            for row in range(own_rows):
                local = tokens[step, group * own_rows + row] - start
                lane = group // 2 * SLOTS + step * own_rows + row
                all_ids = jnp.where((half_of == half) & (lane_of == lane), local, all_ids)
                here = (local >= 0) & (local < shard_rows)
                place = count - turn[0] * ROOM
                now = here & (place >= 0) & (place < ROOM)

                @pl.when(now)
                def _():
                    found[3 * n] = local
                    found[3 * n + 1] = group
                    found[3 * n + 2] = place

                n = n + now.astype(jnp.int32)
                count = count + here.astype(jnp.int32)
        return n, all_ids

    n, all_ids = lax.fori_loop(
        0, rows.shape[0], scan, (jnp.int32(0), jnp.full(ids.shape, -1, jnp.int32))
    )
    ids[...] = all_ids
    copy.wait()

    def give(i, _):
        local, group, place = found[3 * i], found[3 * i + 1], found[3 * i + 2]
        block = held[pl.ds(pl.multiple_of(local // 16 * 16, 16), 16), :]
        row = placed(picked(block, local % 16), place, ROOM)
        rows[group] = (rows[group].astype(jnp.float32) + row).astype(jnp.bfloat16)
        return 0

    lax.fori_loop(0, n, give, 0)


def own_tokens(tokens, own_rows, shard_rows):
    group = lax.axis_index(DP)
    holders, order = [], []
    for step in range(tokens.shape[0]):
        for row in range(own_rows):
            holder = tokens[step, group * own_rows + row] // shard_rows
            order.append(sum(((holder == h).astype(jnp.int32) for h in holders), jnp.int32(0)))
            holders.append(holder)
    return holders, order


def collect_kernel(shard_rows, turn, tokens, rows, out, buffer, sems):
    own_rows = out.shape[1]
    n_vocab = lax.axis_size("vocab")
    holders, order = own_tokens(tokens, own_rows, shard_rows)
    out[...] = jnp.zeros_like(out)
    wanted, copies = [], []
    for i, (holder, place) in enumerate(zip(holders, order)):
        wanted.append(
            (holder % n_vocab == lax.axis_index("vocab")) & (place // ROOM == turn[0])
        )
        copies.append(
            pltpu.make_async_copy(rows.at[holder // n_vocab], buffer.at[i], sems.at[i])
        )
        pl.when(wanted[i])(copies[i].start)
    for i, place in enumerate(order):

        @pl.when(wanted[i])
        def _():
            copies[i].wait()
            row = placed(picked(buffer[i], place % ROOM), i % own_rows, own_rows)
            step = i // own_rows
            out[step] = (out[step].astype(jnp.float32) + row).astype(jnp.bfloat16)


def norm_kernel(shard_rows, tokens, looked, hidden, gain, normed, final, buffer, sems):
    steps, own_rows, _ = looked.shape[1:]
    n_vocab = lax.axis_size("vocab")
    holders, _ = own_tokens(tokens, own_rows, shard_rows)
    copies = []
    for i, holder in enumerate(holders):
        copies.append(
            pltpu.make_async_copy(
                looked.at[holder % n_vocab, i // own_rows], buffer.at[i], sems.at[i]
            )
        )
        copies[i].start()
    current = hidden[...]
    states = []
    for step in range(steps):
        square_mean = jnp.mean(current * current, axis=-1, keepdims=True)
        states.append(current * lax.rsqrt(square_mean + epsilon_value) * gain[...])
        row_of = lax.broadcasted_iota(jnp.int32, current.shape, 0)
        here = jnp.zeros_like(current)
        for row in range(own_rows):
            copies[step * own_rows + row].wait()
            block = buffer[step * own_rows + row].astype(jnp.float32)
            here = jnp.where(row_of == row, block, here)
        current = current + math.sqrt(D) * here
    final[...] = current
    empty = jnp.zeros((SLOTS - steps * own_rows, D), jnp.float32)
    normed[...] = jnp.concatenate([*states, empty], axis=0).astype(jnp.bfloat16)


def on_chip(kernel, out_shape, scratch, *operands):
    return pl.pallas_call(
        kernel,
        out_shape=out_shape,
        in_specs=[pl.BlockSpec(memory_space=space) for _, space in operands],
        out_specs=jax.tree.map(lambda _: pl.BlockSpec(memory_space=pltpu.VMEM), out_shape),
        scratch_shapes=scratch,
        compiler_params=pltpu.CompilerParams(vmem_limit_bytes=20 * 2**20),
    )(*(x for x, _ in operands))


def on_device(hidden, norm_gain, embed_table, tokens):
    own_rows = hidden.shape[0]
    shard_rows = embed_table.shape[0]
    n_xy, n_groups, n_vocab = lax.axis_size(XY), lax.axis_size(DP), lax.axis_size("vocab")
    core = lax.axis_index("dp_2")
    used = STEPS * own_rows
    columns = lax.broadcasted_iota(jnp.int32, (1, shard_rows), 1)
    by_step = jnp.transpose(tokens)
    bf16, f32 = jnp.bfloat16, jnp.float32

    def sent(turn):
        turn = jnp.full((1,), turn, jnp.int32)
        rows, ids = on_chip(
            lookup_kernel,
            (
                jax.ShapeDtypeStruct((n_groups, ROOM, D), bf16),
                jax.ShapeDtypeStruct((2, n_xy * SLOTS), jnp.int32),
            ),
            [
                pltpu.VMEM(embed_table.shape, bf16),
                pltpu.SMEM((3 * n_groups * used,), jnp.int32),
                pltpu.SemaphoreType.DMA,
            ],
            (turn, pltpu.SMEM),
            (by_step, pltpu.SMEM),
            (embed_table, pl.ANY),
        )
        rows = exchange(rows, DP)
        held = on_chip(
            functools.partial(collect_kernel, shard_rows),
            jax.ShapeDtypeStruct((STEPS, own_rows, D), bf16),
            [pltpu.VMEM((used, ROOM, D), bf16), pltpu.SemaphoreType.DMA((used,))],
            (turn, pltpu.SMEM),
            (by_step, pltpu.SMEM),
            (rows, pl.ANY),
        )
        return held, ids

    holder = by_step // shard_rows
    pairs = holder.reshape(STEPS, n_groups, own_rows)
    same = jnp.zeros((STEPS, n_groups, own_rows), jnp.int32)
    for step in range(STEPS):
        for row in range(own_rows):
            same = same + (pairs == pairs[step : step + 1, :, row : row + 1]).astype(jnp.int32)
    turns = (jnp.max(same) + ROOM - 1) // ROOM

    held, ids = sent(0)
    _, held = lax.while_loop(
        lambda state: state[0] < turns,
        lambda state: (state[0] + 1, state[1] + sent(state[0])[0]),
        (jnp.int32(1), held),
    )
    looked = lax.all_gather(held, "vocab")
    normed, final_hidden = on_chip(
        functools.partial(norm_kernel, shard_rows),
        (
            jax.ShapeDtypeStruct((SLOTS, D), bf16),
            jax.ShapeDtypeStruct((own_rows, D), f32),
        ),
        [pltpu.VMEM((used, own_rows, D), bf16), pltpu.SemaphoreType.DMA((used,))],
        (by_step, pltpu.SMEM),
        (looked, pl.ANY),
        (hidden, pltpu.VMEM),
        (norm_gain.reshape(1, D), pltpu.VMEM),
    )
    match_mine = ids[0][:, None] == columns
    match_theirs = ids[1][:, None] == columns

    of_mine = to_each(normed, XY).reshape(n_xy * SLOTS, D)
    of_theirs = other_core(of_mine)

    def totals(rows, match):
        logits = lax.dot_general(
            rows, embed_table, (((1,), (1,)), ((), ())), preferred_element_type=jnp.float32
        )
        capped = softcap_value * jnp.tanh(logits / softcap_value)
        exp_total = jnp.sum(jnp.exp(capped), axis=-1)
        target = jnp.sum(jnp.where(match, capped, 0.0), axis=-1)
        return jnp.stack([exp_total, target])

    for_mine = totals(of_mine, match_mine)
    for_theirs = totals(of_theirs, match_theirs)
    halves = jnp.where(
        core == 0, jnp.stack([for_mine, for_theirs]), jnp.stack([for_theirs, for_mine])
    )
    parts = jnp.broadcast_to(halves[None], (n_xy, *halves.shape))
    part = exchange(parts.reshape(2 * n_xy, *halves.shape[1:]), DP).sum(axis=0)
    whole = to_each(part, "vocab").sum(axis=0)
    log_probs = whole[1] - jnp.log(whole[0])
    log_probs = lax.dynamic_slice_in_dim(log_probs, lax.axis_index(XY) * SLOTS, used)
    return (jnp.transpose(log_probs.reshape(STEPS, own_rows)), final_hidden)


def solution(mesh):
    finer = Mesh(
        mesh.devices.reshape(4, 4, 2, mesh.shape["vocab"]), ("dp_0", "dp_1", "dp_2", "vocab")
    )
    in_specs = (P(DP, None), P(), P(DP_VOCAB, None), P())
    out_specs = (P(DP, None), P(DP, None))
    return jax.shard_map(
        on_device, mesh=finer, in_specs=in_specs, out_specs=out_specs, check_vma=False
    )
```

time: 142 us -> 123 us (0.87)
  blocking collectives: 80.3 us -> 58.3 us
  Pallas kernels: 0 us -> 6.23 us
  other arithmetic: 6.78 us -> 0.76 us
  waiting for transfers between devices: 15.2 us -> 20.9 us
  local copies, waits for them, and re-layouts: 5.08 us -> 3.01 us
  matrix products: 6.5 us -> 4.71 us
    all_to_all x3 -> x2, blocking collectives: 47.7 us -> 25.9 us  [exchange(): return lax.all_to_all(x, axis, split_axis=0, concat_axis=0, tiled=True)]
    all_to_all x1 -> x2, starting transfers between devices: 6.31 us -> 16.6 us  [exchange(): return lax.all_to_all(x, axis, split_axis=0, concat_axis=0, tiled=True)]
    ppermute x2 -> x1, starting transfers between devices: 20.4 us -> 10.2 us  [other_core(): return lax.ppermute(x, 'dp_2', [(0, 1), (1, 0)])]
    all_to_all x1 -> x2, waiting for transfers between devices: 11.4 us -> 20.9 us  [exchange(): return lax.all_to_all(x, axis, split_axis=0, concat_axis=0, tiled=True)]
    pallas_call x0 -> x3, Pallas kernels: none -> 6.23 us  [on_chip(): pl.pallas_call(kernel, out_shape=out_shape, in_specs=[pl.BlockSpec(memory...]
    dot_general x2 -> x0, matrix products: 3.93 us -> none  [rows_of(): jnp.dot(match.astype(jnp.bfloat16), embed_table, preferred_element_type=j...]
    ppermute x2 -> x1, waiting for transfers between devices: 3.79 us -> 0.01 us  [other_core(): return lax.ppermute(x, 'dp_2', [(0, 1), (1, 0)])]
    reduce_sum x3 -> x0, other arithmetic: 2.99 us -> none  [the longest x1 2.08 us: on_device(): exchange(found, XY).astype(jnp.float32).sum(axis=0).astype(jnp.bfloat16)]
  transfers between devices with their start and end apart: 3 -> 3, of which waited for: 3 -> 2; matrix products, arithmetic and copies ran while one was open for 1% -> 5% of each run, Pallas kernels for 0% -> 0%
where the time goes in v3:
time: 123 us; the launch traced here: 122 us
  blocking collectives  58.3 us (47%)
  starting transfers between devices  26.8 us (22%)
  waiting for transfers between devices  20.9 us (17%)
  Pallas kernels  6.23 us (5%)
  matrix products  4.71 us (4%)
  local copies, waits for them, and re-layouts  3.01 us (2%)
  between operations  1.53 us (1%)
    all_gather x1, blocking collectives, on_device(): looked = lax.all_gather(held, 'vocab')  32.3 us
    all_to_all x2, blocking collectives, exchange(): return lax.all_to_all(x, axis, split_axis=0, concat_axis=0, tiled=True)  25.9 us
    all_to_all x2, waiting for transfers between devices, exchange(): return lax.all_to_all(x, axis, split_axis=0, concat_axis=0, tiled=True)  20.9 us
    all_to_all x2, starting transfers between devices, exchange(): return lax.all_to_all(x, axis, split_axis=0, concat_axis=0, tiled=True)  16.6 us
    ppermute x1, starting transfers between devices, other_core(): return lax.ppermute(x, 'dp_2', [(0, 1), (1, 0)])  10.2 us
    pallas_call x3, Pallas kernels, on_chip(): pl.pallas_call(kernel, out_shape=out_shape, in_specs=[pl.BlockSpec(memory...  6.23 us
    dot_general x2, matrix products, totals(): lax.dot_general(rows, embed_table, (((1,), (1,)), ((), ())), preferred_el...  4.71 us
  transfers between devices with their start and end apart: 3, of which 2 were waited for; matrix products, arithmetic and copies ran while one was open for 5% of the time, Pallas kernels for 0%

profile of v3, /device:TPU:1, one launch (start us, length us, event | category | flops | bytes accessed | tf_op | source)
XLA Modules:
  0.0 122.3 jit_solution(3560439545805478403)
XLA Ops:
  0.6 3.5 %shard_map.59 = (bf16[32,2,4608]{2,1,0:T(2,128)(2,1)}, s32[2,128]{1,0:T(2,128)S(1)}) custom-call(s32[1]{0:T(128)} %constant.49.clone.1.turn, s32[3,64]{1,0:T(4,128)} %bitcast.32, bf16[384,4608]{1,0:T(8,128)(2,1)} %table.1), custom_call_target="tpu_custom_call" | custom-call | tf_op jit(solution)/shard_map/pallas_call | solution.py:164
  4.1 0.0 copy-start.2
  4.2 0.0 copy-start.3
  4.2 10.6 %all-to-all-start.1 = ((bf16[32,2,4608]{2,1,0:T(2,128)(2,1)}), bf16[32,2,4608]{2,1,0:T(2,128)(2,1)S(1)}, u32[]{:S(2)}, u32[]{:S(2)}) async-start(bf16[32,2,4608]{2,1,0:T(2,128)(2,1)} %get-tuple-element.35), calls=%async_computation.1 | async-start | bytes 1179648 | tf_op jit(solution)/shard_map/all_to_all | solution.py:25
  14.8 0.0 copy-done.2
  14.8 0.1 reshape.66
  14.9 0.3 slice_reduce_fusion.5
  15.2 0.1 eq.125
  15.3 0.1 eq.126
  15.4 0.1 eq.130
  15.5 0.1 eq.131
  15.6 0.1 eq.135
  15.6 0.1 eq.136
  15.8 0.1 eq.140
  15.8 0.1 eq.141
  15.9 0.1 eq.145
  16.0 0.1 eq.146
  16.1 0.1 eq.150
  16.2 0.1 eq.151
  16.3 0.7 add_reduce_fusion
  17.6 0.0 copy-done.3
  17.7 9.5 %all-to-all-done.1.rows = bf16[32,2,4608]{2,1,0:T(2,128)(2,1)S(1)} async-done(((bf16[32,2,4608]{2,1,0:T(2,128)(2,1)}), bf16[32,2,4608]{2,1,0:T(2,128)(2,1)S(1)}, u32[]{:S(2)}, u32[]{:S(2)}) %all-to-all-start.1) | async-done | bytes 589856 | tf_op jit(solution)/shard_map/all_to_all | solution.py:25
  27.2 0.8 shard_map.60
  28.0 0.0 copy-start
  28.0 32.3 %all-gather = bf16[48,2,4608]{2,1,0:T(2,128)(2,1)S(1)} all-gather(bf16[3,2,4608]{2,1,0:T(2,128)(2,1)S(1)} %get-tuple-element.36), channel_id=2, replica_groups=mesh['dp_0'=4,'dp_1'=4,'dp_2'=2,'vocab'=16] {'vocab'}, dimensions={0}, use_global_device_ids=true | all-gather | bytes 940032 | tf_op jit(solution)/shard_map/all_gather | solution.py:226
  60.3 0.0 copy-done
  60.3 1.9 %shard_map.61 = (bf16[8,4608]{1,0:T(8,128)(2,1)S(1)}, f32[2,4608]{1,0:T(2,128)}) custom-call(s32[3,64]{1,0:T(4,128)S(1)} %get-tuple-element.133, bf16[16,3,2,4608]{3,2,1,0:T(2,128)(2,1)S(1)} %bitcast.30, f32[2,4608]{1,0:T(2,128)S(1)} %copy-done, f32[1,4608]{1,0:T(1,128)S(1)} %reshape.67.gain), custom_call_target="tpu_custom_call" | custom-call | tf_op jit(solution)/shard_map/pallas_call | solution.py:164
  62.3 0.1 broadcast_in_dim.14
  62.4 15.1 %all_to_all.26 = bf16[16,8,4608]{2,1,0:T(8,128)(2,1)S(1)} all-to-all(bf16[16,8,4608]{2,1,0:T(8,128)(2,1)S(1)} %broadcast_in_dim.14), channel_id=1, replica_groups=mesh['dp_0'=4,'dp_1'=4,'dp_2'=2,'vocab'=16] {'dp_0','dp_1'}, dimensions={0} | all-to-all | bytes 2359296 | tf_op jit(solution)/shard_map/all_to_all | solution.py:25
  77.5 10.2 %collective-permute-start = (bf16[128,4608]{1,0:T(8,128)(2,1)S(1)}, bf16[128,4608]{1,0:T(8,128)(2,1)S(1)}, u32[]{:S(2)}, u32[]{:S(2)}) collective-permute-start(bf16[128,4608]{1,0:T(8,128)(2,1)S(1)} %bitcast.31), channel_id=1, source_target_pairs={{0,16},{16,0},{1,17},{17,1},{2,18},{18,2},{3,19},{19,3},{4,20},{20... | collective-permute-start | bytes 3538952 | tf_op jit(solution)/shard_map/ppermute | solution.py:33
  87.8 0.0 copy-start.1
  87.8 3.4 %exponential_reduce_fusion.1 = (f32[128]{0:T(128)S(1)}, f32[128]{0:T(128)S(1)}) fusion(s32[128]{0:T(128)S(1)} %get-tuple-element.72, bf16[384,4608]{1,0:T(8,128)(2,1)} %get-tuple-element.130, bf16[16,8,4608]{2,1,0:T(8,128)(2,1)S(1)} %all_to_all.26), kind=kOutput, calls=%fused_computation.11 | convolution fusion | flops 453279488 | bytes 4720128 | tf_op jit(solution)/shard_map/dot_general | solution.py:246
  91.2 0.0 collective-permute-done
  91.2 0.0 copy-done.1
  91.2 1.3 %exponential_reduce_fusion = (f32[128]{0:T(128)S(1)}, f32[128]{0:T(128)S(1)}) fusion(s32[128]{0:T(128)S(1)} %get-tuple-element.73, bf16[128,4608]{1,0:T(8,128)(2,1)S(1)} %collective-permute-done, bf16[384,4608]{1,0:T(8,128)(2,1)S(1)} %copy-done.1), kind=kOutput, calls=%fused_computation.8 | convolution fusion | flops 453279488 | bytes 4720128 | tf_op jit(solution)/shard_map/dot_general | solution.py:246
  92.6 10.8 %all_to_all.27 = f32[32,2,128]{2,1,0:T(2,128)S(1)} all-to-all(f32[32,2,128]{2,1,0:T(2,128)S(1)} %bitcast.35), channel_id=1, replica_groups=mesh['dp_0'=4,'dp_1'=4,'dp_2'=2,'vocab'=16] {'dp_0','dp_1','dp_2'}, dimensions={0} | all-to-all | bytes 65536 | tf_op jit(solution)/shard_map/all_to_all | solution.py:25
  103.4 0.6 broadcast_in_dim.29
  104.0 6.0 %all-to-all-start.4 = ((f32[16,2,128]{2,1,0:T(2,128)}), f32[16,2,128]{2,1,0:T(2,128)S(1)}, u32[]{:S(2)}, u32[]{:S(2)}) async-start(f32[16,2,128]{2,1,0:T(2,128)} %broadcast_in_dim.29), calls=%async_computation.4 | async-start | bytes 32768 | tf_op jit(solution)/shard_map/all_to_all | solution.py:25
  110.0 11.4 %all-to-all-done.4 = f32[16,2,128]{2,1,0:T(2,128)S(1)} async-done(((f32[16,2,128]{2,1,0:T(2,128)}), f32[16,2,128]{2,1,0:T(2,128)S(1)}, u32[]{:S(2)}, u32[]{:S(2)}) %all-to-all-start.4) | async-done | bytes 16416 | tf_op jit(solution)/shard_map/all_to_all | solution.py:25
  121.4 0.1 dynamic-slice_reduce_fusion
  121.5 0.1 reshape.70
  121.6 0.7 copy.20
  (10 shorter events, 0.1 us)
Async XLA Ops:
  4.1 10.7 %copy-start.2 = (s32[64,3]{0,1:T(4,128)S(1)}, s32[64,3]{0,1:T(4,128)}, u32[]{:S(2)}) copy-start(s32[64,3]{0,1:T(4,128)} %param.9) | copy-start | bytes 2308
  4.2 13.5 %copy-start.3 = (f32[4608]{0:T(1024)S(1)}, f32[4608]{0:T(1024)}, u32[]{:S(2)}) copy-start(f32[4608]{0:T(1024)} %param.7) | copy-start | bytes 55300
  4.2 23.0 %all-to-all-start.1 = ((bf16[32,2,4608]{2,1,0:T(2,128)(2,1)}), bf16[32,2,4608]{2,1,0:T(2,128)(2,1)S(1)}, u32[]{:S(2)}, u32[]{:S(2)}) async-start(bf16[32,2,4608]{2,1,0:T(2,128)(2,1)} %get-tuple-element.35), calls=%async_computation.1 | async-start | bytes 1179648 | tf_op jit(solution)/shard_map/all_to_all | solution.py:25
  28.0 32.4 %copy-start = (f32[2,4608]{1,0:T(2,128)S(1)}, f32[2,4608]{1,0:T(2,128)}, u32[]{:S(2)}) copy-start(f32[2,4608]{1,0:T(2,128)} %hidden.1) | copy-start | bytes 110596
  77.5 13.7 %collective-permute-start = (bf16[128,4608]{1,0:T(8,128)(2,1)S(1)}, bf16[128,4608]{1,0:T(8,128)(2,1)S(1)}, u32[]{:S(2)}, u32[]{:S(2)}) collective-permute-start(bf16[128,4608]{1,0:T(8,128)(2,1)S(1)} %bitcast.31), channel_id=1, source_target_pairs={{0,16},{16,0},{1,17},{17,1},{2,18},{18,2},{3,19},{19,3},{4,20},{20... | collective-permute-start | bytes 3538952 | tf_op jit(solution)/shard_map/ppermute | solution.py:33
  87.8 3.5 %copy-start.1 = (bf16[384,4608]{1,0:T(8,128)(2,1)S(1)}, bf16[384,4608]{1,0:T(8,128)(2,1)}, u32[]{:S(2)}) copy-start(bf16[384,4608]{1,0:T(8,128)(2,1)} %get-tuple-element.130) | copy-start | bytes 10616836
  104.0 17.4 %all-to-all-start.4 = ((f32[16,2,128]{2,1,0:T(2,128)}), f32[16,2,128]{2,1,0:T(2,128)S(1)}, u32[]{:S(2)}, u32[]{:S(2)}) async-start(f32[16,2,128]{2,1,0:T(2,128)} %broadcast_in_dim.29), calls=%async_computation.4 | async-start | bytes 32768 | tf_op jit(solution)/shard_map/all_to_all | solution.py:25

commit v4 on v2

v4 whole, which is shorter than its diff:
```python
import functools
import math

import jax
import jax.numpy as jnp
from jax import lax
from jax.experimental import pallas as pl
from jax.experimental.pallas import tpu as pltpu
from jax.sharding import Mesh
from jax.sharding import PartitionSpec as P

D = 4608
STEPS = 3
XY = ("dp_0", "dp_1")
DP = ("dp_0", "dp_1", "dp_2")
DP_VOCAB = ("dp_0", "dp_1", "dp_2", "vocab")
PIECES = 4
SLOTS = 8

epsilon_value = 1e-06
softcap_value = 30.0


def exchange(x, axis):
    return lax.all_to_all(x, axis, split_axis=0, concat_axis=0, tiled=True)


def to_each(x, axis):
    return exchange(jnp.broadcast_to(x[None], (lax.axis_size(axis), *x.shape)), axis)


def other_core(x):
    return lax.ppermute(x, "dp_2", [(0, 1), (1, 0)])


def holder_of(token, shard_rows, n_devices):
    low = (shard_rows & -shard_rows).bit_length() - 1
    odd, limit = shard_rows >> low, shard_rows * n_devices >> low
    for shift in range(24):
        factor = (1 << shift) // odd + 1
        if limit * factor < 2**31 and all(
            x * factor >> shift == x // odd for x in range(limit + 1)
        ):
            return ((token >> low) * factor) >> shift
    return lax.div(token, jnp.full_like(token, shard_rows))


def parted(x, n):
    if n & (n - 1) == 0:
        return x >> (n.bit_length() - 1), x & (n - 1)
    n = jnp.full_like(x, n)
    return lax.div(x, n), lax.rem(x, n)


def key_of(holder, index, summary, own_rows, n_vocab):
    core = parted(summary, own_rows)[0] & 1
    return ((core * n_vocab + parted(holder, n_vocab)[1]) << 8) + index


def picked(block, index):
    rows = lax.broadcasted_iota(jnp.int32, block.shape, 0)
    return jnp.sum(jnp.where(rows == index, block.astype(jnp.float32), 0.0), axis=0, keepdims=True)


def placed(row, index, count):
    rows = lax.broadcasted_iota(jnp.int32, (count, row.shape[1]), 0)
    return jnp.where(rows == index, row, 0.0)


def in_pieces(row):
    width = row.shape[1] // PIECES
    parts = [placed(row[:, i * width : (i + 1) * width], i, PIECES) for i in range(PIECES)]
    return sum(parts[1:], parts[0])


def in_row(block):
    return jnp.concatenate([picked(block, i) for i in range(PIECES)], axis=1)


def split(hidden, out):
    count = hidden.shape[0]
    total = jnp.zeros((SLOTS, D), jnp.float32)
    rest = jnp.zeros((SLOTS, D // PIECES), jnp.float32)
    for row in range(count):
        state = hidden[row : row + 1, :]
        high = state.astype(jnp.bfloat16).astype(jnp.float32)
        total = total + placed(high, SLOTS - count + row, SLOTS)
        pieces = jnp.concatenate([in_pieces(state - high)] * (SLOTS // PIECES), axis=0)
        at = lax.broadcasted_iota(jnp.int32, pieces.shape, 0) // PIECES
        rest = rest + jnp.where(at == row, pieces, 0.0)
    out[:, :D] = total.astype(jnp.bfloat16)
    out[:, D:] = rest.astype(jnp.bfloat16)


def lookup_kernel(
    turn, tokens, tokens_again, hidden, table, rows, packed, rank_out, slots, held, found, sem
):
    steps, summaries = tokens.shape
    shard_rows, n_groups, n_vocab = table.shape[0], rows.shape[0], lax.axis_size("vocab")
    n_devices, own_rows = n_groups * n_vocab, hidden.shape[0]
    lines, vocab = n_groups // 2, lax.axis_index("vocab")
    start = (lax.axis_index(DP) * n_vocab + vocab) * shard_rows
    copy = pltpu.make_async_copy(table, held, sem)
    copy.start()
    rows[...] = jnp.zeros_like(rows)
    split(hidden, packed)
    summary_of = lax.broadcasted_iota(jnp.int32, tokens.shape, 1)
    index_of = lax.broadcasted_iota(jnp.int32, tokens.shape, 0) * summaries + summary_of
    holders = holder_of(tokens_again[...], shard_rows, n_devices)
    keys = key_of(holders, index_of, summary_of, own_rows, n_vocab)

    def scan(summary, state):
        n, rank, among = state
        for step in range(steps):
            token, index = tokens[step, summary], step * summaries + summary
            local = token - start
            found[n] = index
            n = n + ((local >= 0) & (local < shard_rows)).astype(jnp.int32)
            holder = holder_of(token, shard_rows, n_devices)
            key = key_of(holder, index, summary, own_rows, n_vocab)
            before = key < keys
            rank = rank + jnp.where(before, 1, 0)
            among = among + jnp.where(before & ((key ^ keys) < 256), 1, 0)
        return n, rank, among

    none = jnp.zeros(tokens.shape, jnp.int32)
    n, rank, among = lax.fori_loop(0, summaries, scan, (jnp.int32(0), none, none))
    rank_out[...] = rank
    turns = parted(among, lines)[0]
    first = lax.axis_index("dp_2") * (steps * summaries // 2) + lax.axis_index(XY)
    for i in range(slots.shape[1]):
        hit = rank == first + i * lines
        slots[0, i] = jnp.sum(jnp.where(hit, holders, 0))
        slots[1, i] = jnp.sum(jnp.where(hit, turns, 0))
        slots[2, i] = jnp.int32(0)
    slots[2, 0] = jnp.max(turns) + 1
    copy.wait()

    def give(i, _):
        index = found[i]
        step, summary = parted(index, summaries)
        local = tokens[step, summary] - start
        core = parted(summary, own_rows)[0] & 1
        at = index_of == index
        its_rank = jnp.sum(jnp.where(at, rank, 0)) - core * (steps * summaries // 2)
        its_turn = jnp.sum(jnp.where(at, turns, 0))

        @pl.when(its_turn == turn[0])
        def _():
            block = held[pl.ds(pl.multiple_of(local // 16 * 16, 16), 16), :]
            row = in_pieces(picked(block, local % 16))
            rows[parted(its_rank, lines)[1] * 2 + core] = row.astype(jnp.bfloat16)

        return 0

    lax.fori_loop(0, n, give, 0)


def relay_kernel(turn, slots, rows, out, buffer, sem):
    n_vocab = out.shape[0]
    out[...] = jnp.zeros_like(out)
    for i in range(slots.shape[1]):

        @pl.when((slots[0, i] % n_vocab == lax.axis_index("vocab")) & (slots[1, i] == turn[0]))
        def _():
            copy = pltpu.make_async_copy(rows.at[slots[0, i] // n_vocab], buffer, sem)
            copy.start()
            copy.wait()
            out[...] = jnp.broadcast_to(buffer[...][None], out.shape)


def pack_kernel(turn, slots, rows, before, out):
    total = before[:, :D].astype(jnp.float32)
    for i in range(slots.shape[1]):
        row = in_row(rows[slots[0, i] % rows.shape[0]])
        total = total + placed(row, jnp.where(slots[1, i] == turn[0], i, -1), out.shape[0])
    out[:, :D] = total.astype(jnp.bfloat16)
    out[:, D:] = before[:, D:]


def head_kernel(rows, own_hidden, gain, places, table, out, *more):
    *final, gain_in, places_in, held, normed, sems = more
    final = final[0] if final else None
    copies = [
        pltpu.make_async_copy(x, y, sems.at[i])
        for i, (x, y) in enumerate([(places, places_in), (gain, gain_in), (table, held)])
    ]
    for copy in copies:
        copy.start()
    own_rows = own_hidden.shape[0]
    count = rows.shape[0] // SLOTS * own_rows
    steps = normed.shape[0] // count
    at = lax.broadcasted_iota(jnp.int32, (rows.shape[0], count), 0)
    state = lax.broadcasted_iota(jnp.int32, (rows.shape[0], count), 1)
    block, state = state // own_rows * SLOTS, state % own_rows

    def taken(chosen, columns):
        return lax.dot_general(
            jnp.where(chosen, 1.0, 0.0).astype(jnp.bfloat16), rows[:, columns],
            (((0,), (0,)), ((), ())), preferred_element_type=jnp.float32,
        )

    high = taken(at == block + SLOTS - own_rows + state, slice(0, D))
    low = [
        taken(at == block + state * PIECES + i, slice(D, D + D // PIECES)) for i in range(PIECES)
    ]
    hidden = high + jnp.concatenate(low, axis=1)
    copies[0].wait()

    def looked_up(row, n):
        at = lax.broadcasted_iota(jnp.int32, (rows.shape[0], n), 0)
        return taken(at == places_in[row : row + 1, :n], slice(0, D))

    looked = looked_up(0, (steps - 1) * count)
    copies[1].wait()
    current = hidden
    for step in range(steps):
        square_mean = jnp.mean(current * current, axis=-1, keepdims=True)
        state = current * lax.rsqrt(square_mean + epsilon_value) * gain_in[...]
        normed[pl.ds(step * count, count), :] = state.astype(jnp.bfloat16)
        if step < steps - 1:
            current = current + math.sqrt(D) * looked[step * count : (step + 1) * count]
    copies[2].wait()
    logits = lax.dot_general(
        held[...], normed[...], (((1,), (1,)), ((), ())), preferred_element_type=jnp.float32
    )
    capped = softcap_value * jnp.tanh(logits / softcap_value)
    exp_total = jnp.sum(jnp.exp(capped), axis=0, keepdims=True)
    entry = lax.broadcasted_iota(jnp.int32, capped.shape, 0)
    ids = places_in[1:2, : steps * count]
    target = jnp.sum(jnp.where(entry == ids, capped, 0.0), axis=0, keepdims=True)
    out[...] = jnp.concatenate([exp_total, target], axis=0)
    if final is None:
        return
    own = looked_up(2, SLOTS)
    current = own_hidden[...]
    for step in range(steps):
        current = current + math.sqrt(D) * own[step * own_rows : (step + 1) * own_rows]
    final[...] = current


def on_chip(kernel, out_shape, scratch, *operands):
    operands = [x if isinstance(x, tuple) else (x, pltpu.VMEM) for x in operands]
    return pl.pallas_call(
        kernel,
        out_shape=out_shape,
        in_specs=[pl.BlockSpec(memory_space=space) for _, space in operands],
        out_specs=jax.tree.map(
            lambda x: pl.BlockSpec(memory_space=pltpu.SMEM if x.shape[0] == 3 and x.shape[1] < SLOTS else pltpu.VMEM),
            out_shape,
        ),
        scratch_shapes=scratch,
        compiler_params=pltpu.CompilerParams(vmem_limit_bytes=24 * 2**20),
    )(*(x for x, _ in operands))


def on_device(hidden, norm_gain, embed_table, tokens):
    own_rows = hidden.shape[0]
    shard_rows = embed_table.shape[0]
    n_xy, n_groups, n_vocab = lax.axis_size(XY), lax.axis_size(DP), lax.axis_size("vocab")
    chip, core, summaries = lax.axis_index(XY), lax.axis_index("dp_2"), tokens.shape[0]
    start = (lax.axis_index(DP) * n_vocab + lax.axis_index("vocab")) * shard_rows
    half = summaries // 2
    bf16, f32, i32 = jnp.bfloat16, jnp.float32, jnp.int32
    by_step = jnp.transpose(tokens)
    row_shape = (PIECES, D // PIECES)

    per_half = STEPS * half
    n_slots = per_half // n_xy

    def lookup(turn):
        return on_chip(
            lookup_kernel,
            (
                jax.ShapeDtypeStruct((n_groups, *row_shape), bf16),
                jax.ShapeDtypeStruct((SLOTS, D + D // PIECES), bf16),
                jax.ShapeDtypeStruct(by_step.shape, i32),
                jax.ShapeDtypeStruct((3, n_slots), i32),
            ),
            [
                pltpu.VMEM(embed_table.shape, bf16),
                pltpu.SMEM((STEPS * summaries + 1,), i32),
                pltpu.SemaphoreType.DMA,
            ],
            (turn, pltpu.SMEM),
            (by_step, pltpu.SMEM),
            by_step,
            hidden,
            (embed_table, pl.ANY),
        )

    first = jnp.zeros((1,), i32)
    rows, packed, rank, slots = lookup(first)
    turns = slots[2, 0]
    rows = exchange(rows, DP)

    def relay(turn, rows):
        return on_chip(
            relay_kernel,
            jax.ShapeDtypeStruct((n_vocab, *row_shape), bf16),
            [pltpu.VMEM(row_shape, bf16), pltpu.SemaphoreType.DMA],
            (turn, pltpu.SMEM),
            (slots, pltpu.SMEM),
            (rows, pl.ANY),
        )

    def pack(turn, rows, packed):
        return on_chip(
            pack_kernel,
            jax.ShapeDtypeStruct(packed.shape, bf16),
            [],
            (turn, pltpu.SMEM),
            (slots, pltpu.SMEM),
            rows,
            packed,
        )

    rows = relay(first, rows)
    rows, rank, flat, gain = lax.optimization_barrier((rows, rank, by_step, norm_gain))
    rows = exchange(rows, "vocab")
    gain = gain.reshape(1, D)

    def halves(x):
        x = jnp.transpose(x.reshape(STEPS, n_xy, 2, own_rows), (2, 0, 1, 3)).reshape(2, per_half)
        return jnp.where(core == 0, x, x[::-1])

    place = rank - jnp.where(rank < per_half, 0, per_half)
    slot, line = parted(place, n_xy)
    place = halves(line * SLOTS + slot)
    own = lax.dynamic_slice_in_dim(
        place[0].reshape(STEPS, half), chip * own_rows, own_rows, 1
    ).reshape(1, STEPS * own_rows)
    wide = n_xy * SLOTS

    def widened(x):
        return jnp.pad(x, ((0, 0), (0, wide - x.shape[1])), constant_values=-1)

    own = widened(jnp.concatenate([own, own]).reshape(2, -1)[:, : STEPS * own_rows])
    places = jnp.stack(
        [widened(place[:, : 2 * half]), widened(halves(flat - start)), own, own], axis=1
    )
    places_mine, places_theirs = places[0], places[1]
    rows, places_mine, places_theirs, gain = lax.optimization_barrier(
        (rows, places_mine, places_theirs, gain)
    )

    def further(state):
        turn = state[0][None]
        rows = exchange(relay(turn, exchange(lookup(turn)[0], DP)), "vocab")
        return state[0] + 1, pack(turn, rows, state[1])

    _, packed = lax.while_loop(
        lambda state: state[0] < turns, further, (jnp.int32(1), pack(first, rows, packed))
    )
    of_mine = to_each(packed, XY).reshape(wide, D + D // PIECES)
    of_theirs = other_core(of_mine)

    def totals(rows, places, *more):
        return on_chip(
            head_kernel,
            (jax.ShapeDtypeStruct((2, per_half), f32), *more),
            [
                pltpu.VMEM((1, D), f32),
                pltpu.VMEM(places.shape, i32),
                pltpu.VMEM(embed_table.shape, bf16),
                pltpu.VMEM((per_half, D), bf16),
                pltpu.SemaphoreType.DMA((3,)),
            ],
            rows,
            hidden,
            (gain, pl.ANY),
            (places, pl.ANY),
            (embed_table, pl.ANY),
        )

    for_mine, final_hidden = totals(
        of_mine, places_mine, jax.ShapeDtypeStruct(hidden.shape, f32)
    )
    (for_theirs,) = totals(of_theirs, places_theirs)

    both = jnp.where(
        core == 0, jnp.stack([for_mine, for_theirs]), jnp.stack([for_theirs, for_mine])
    )
    parts = jnp.broadcast_to(both[None], (n_xy, *both.shape))
    part = exchange(parts.reshape(2 * n_xy, *both.shape[1:]), DP).sum(axis=0)
    whole = to_each(part, "vocab").sum(axis=0)
    log_probs = (whole[1] - jnp.log(whole[0])).reshape(STEPS, half)
    log_probs = lax.dynamic_slice_in_dim(log_probs, chip * own_rows, own_rows, 1)
    return (jnp.transpose(log_probs), final_hidden)


def solution(mesh):
    finer = Mesh(
        mesh.devices.reshape(4, 4, 2, mesh.shape["vocab"]), ("dp_0", "dp_1", "dp_2", "vocab")
    )
    in_specs = (P(DP, None), P(), P(DP_VOCAB, None), P())
    out_specs = (P(DP, None), P(DP, None))
    return jax.shard_map(
        on_device, mesh=finer, in_specs=in_specs, out_specs=out_specs, check_vma=False
    )
```

time: 142 us -> 118 us (0.83)
  blocking collectives: 80.3 us -> 50.2 us
  Pallas kernels: 0 us -> 12.3 us
  other arithmetic: 6.78 us -> 0.15 us
  matrix products: 6.5 us -> 0 us
  waiting for transfers between devices: 15.2 us -> 21.4 us
  starting transfers between devices: 26.7 us -> 29.7 us
  local copies, waits for them, and re-layouts: 5.08 us -> 2.39 us
    all_gather x1 -> x0, blocking collectives: 32.5 us -> none  [on_device(): looked = lax.all_gather(held[:used].reshape(STEPS, own_rows, D), 'vocab')]
    all_to_all x1 -> x2, starting transfers between devices: 6.31 us -> 23.6 us  [exchange(): return lax.all_to_all(x, axis, split_axis=0, concat_axis=0, tiled=True)]
    ppermute x2 -> x1, starting transfers between devices: 20.4 us -> 6.1 us  [other_core(): return lax.ppermute(x, 'dp_2', [(0, 1), (1, 0)])]
    pallas_call x0 -> x5, Pallas kernels: none -> 12.3 us  [on_chip(): pl.pallas_call(kernel, out_shape=out_shape, in_specs=[pl.BlockSpec(memory...]
    all_to_all x1 -> x2, waiting for transfers between devices: 11.4 us -> 21.4 us  [exchange(): return lax.all_to_all(x, axis, split_axis=0, concat_axis=0, tiled=True)]
    dot_general x4 -> x0, matrix products: 6.5 us -> none  [the longest x2 3.93 us: rows_of(): jnp.dot(match.astype(jnp.bfloat16), embed_table, preferred_element_type=j...]
    ppermute x2 -> x1, waiting for transfers between devices: 3.79 us -> 0.01 us  [other_core(): return lax.ppermute(x, 'dp_2', [(0, 1), (1, 0)])]
    reduce_sum x4 -> x1, other arithmetic: 3.79 us -> 0.04 us  [on_device(): part = exchange(parts.reshape(2 * n_xy, *both.shape[1:]), DP).sum(axis=0)]
  transfers between devices with their start and end apart: 3 -> 3, of which waited for: 3 -> 2; matrix products, arithmetic and copies ran while one was open for 1% -> 1% of each run, Pallas kernels for 0% -> 3%
where the time goes in v4:
time: 118 us
  blocking collectives  50.2 us (43%)
  starting transfers between devices  29.7 us (25%)
  waiting for transfers between devices  21.4 us (18%)
  Pallas kernels  12.3 us (10%)
  local copies, waits for them, and re-layouts  2.39 us (2%)
    all_to_all x3, blocking collectives, exchange(): return lax.all_to_all(x, axis, split_axis=0, concat_axis=0, tiled=True)  50.2 us
    all_to_all x2, starting transfers between devices, exchange(): return lax.all_to_all(x, axis, split_axis=0, concat_axis=0, tiled=True)  23.6 us
    all_to_all x2, waiting for transfers between devices, exchange(): return lax.all_to_all(x, axis, split_axis=0, concat_axis=0, tiled=True)  21.4 us
    pallas_call x5, Pallas kernels, on_chip(): pl.pallas_call(kernel, out_shape=out_shape, in_specs=[pl.BlockSpec(memory...  12.3 us
    ppermute x1, starting transfers between devices, other_core(): return lax.ppermute(x, 'dp_2', [(0, 1), (1, 0)])  6.1 us
  transfers between devices with their start and end apart: 3, of which 2 were waited for; matrix products, arithmetic and copies ran while one was open for 1% of the time, Pallas kernels for 3%

profile of v4, /device:TPU:1, one launch (start us, length us, event | category | flops | bytes accessed | tf_op | source)
XLA Modules:
  0.0 117.7 jit_solution(2370421016624681367)
XLA Ops:
  0.6 0.0 copy-start.2
  0.6 3.6 %shard_map.59 = (bf16[32,4,1152]{2,1,0:T(4,128)(2,1)}, bf16[8,5760]{1,0:T(8,128)(2,1)S(1)}, s32[3,64]{1,0:T(4,128)S(1)}, s32[3,6]{1,0:T(4,128)S(1)}) custom-call(s32[1]{0:T(128)} %constant.9.clone.1.turn, s32[3,64]{1,0:T(4,128)} %bitcast.31, s32[3,64]{1,0:T(4,128)} %bitcast.32, f32[2,4608]{1,0:T(2,128)} %own_hidden.3, bf16[384,4608]{1,0:T(8,128)(2,1)} %table.5), custom_call_target="tpu_custom_call" | custom-call | tf_op jit(solution)/shard_map/pallas_call | solution.py:244
  4.2 0.0 copy-start.3
  4.2 0.0 copy-start.1
  4.2 10.8 %all-to-all-start.2 = ((bf16[32,4,1152]{2,1,0:T(4,128)(2,1)}), bf16[32,4,1152]{2,1,0:T(4,128)(2,1)S(1)}, u32[]{:S(2)}, u32[]{:S(2)}) async-start(bf16[32,4,1152]{2,1,0:T(4,128)(2,1)} %get-tuple-element.56), calls=%async_computation.2 | async-start | bytes 589824 | tf_op jit(solution)/shard_map/all_to_all | solution.py:25
  15.1 0.6 slice.25
  15.7 8.8 %all-to-all-done.2.rows = bf16[32,4,1152]{2,1,0:T(4,128)(2,1)S(1)} async-done(((bf16[32,4,1152]{2,1,0:T(4,128)(2,1)}), bf16[32,4,1152]{2,1,0:T(4,128)(2,1)S(1)}, u32[]{:S(2)}, u32[]{:S(2)}) %all-to-all-start.2) | async-done | bytes 294944 | tf_op jit(solution)/shard_map/all_to_all | solution.py:25
  24.5 1.3 %shard_map.60 = bf16[16,4,1152]{2,1,0:T(4,128)(2,1)} custom-call(s32[1]{0:T(128)} %constant.9.clone.1.turn, s32[3,6]{1,0:T(4,128)S(1)} %get-tuple-element.148.slots, bf16[32,4,1152]{2,1,0:T(4,128)(2,1)S(1)} %all-to-all-done.2.rows), custom_call_target="tpu_custom_call" | custom-call | tf_op jit(solution)/shard_map/pallas_call | solution.py:244
  25.8 0.0 copy-done.2
  25.9 0.1 reshape.68
  26.0 0.1 reshape.69
  26.2 0.1 reshape_squeeze.3
  26.3 0.1 constant_dynamic-slice_fusion
  26.3 0.1 reshape.72
  26.4 0.1 reshape.70
  26.6 0.1 reshape.71
  26.8 12.8 %all-to-all-start.3 = ((bf16[16,4,1152]{2,1,0:T(4,128)(2,1)}), bf16[16,4,1152]{2,1,0:T(4,128)(2,1)S(1)}, u32[]{:S(2)}, u32[]{:S(2)}) async-start(bf16[16,4,1152]{2,1,0:T(4,128)(2,1)} %shard_map.60), calls=%async_computation.3 | async-start | bytes 294912 | tf_op jit(solution)/shard_map/all_to_all | solution.py:25
  39.6 0.0 copy-done.3
  39.7 12.5 %all-to-all-done.3.rows = bf16[16,4,1152]{2,1,0:T(4,128)(2,1)S(1)} async-done(((bf16[16,4,1152]{2,1,0:T(4,128)(2,1)}), bf16[16,4,1152]{2,1,0:T(4,128)(2,1)S(1)}, u32[]{:S(2)}, u32[]{:S(2)}) %all-to-all-start.3) | async-done | bytes 147488 | tf_op jit(solution)/shard_map/all_to_all | solution.py:25
  52.2 0.9 shard_map.61
  53.1 0.0 copy-done.1
  53.1 0.6 while.10
  53.8 0.0 copy-start
  53.8 0.1 broadcast_in_dim.16
  53.9 21.2 %all_to_all.37 = bf16[16,8,5760]{2,1,0:T(8,128)(2,1)S(1)} all-to-all(bf16[16,8,5760]{2,1,0:T(8,128)(2,1)S(1)} %broadcast_in_dim.16), channel_id=1, replica_groups=mesh['dp_0'=4,'dp_1'=4,'dp_2'=2,'vocab'=16] {'dp_0','dp_1'}, dimensions={0} | all-to-all | bytes 2949120 | tf_op jit(solution)/shard_map/all_to_all | solution.py:25
  75.1 6.1 %collective-permute-start = (bf16[128,5760]{1,0:T(8,128)(2,1)S(1)}, bf16[128,5760]{1,0:T(8,128)(2,1)S(1)}, u32[]{:S(2)}, u32[]{:S(2)}) collective-permute-start(bf16[128,5760]{1,0:T(8,128)(2,1)S(1)} %bitcast.27), channel_id=1, source_target_pairs={{0,16},{16,0},{1,17},{17,1},{2,18},{18,2},{3,19},{19,3},{4,20},{20... | collective-permute-start | bytes 4423688 | tf_op jit(solution)/shard_map/ppermute | solution.py:33
  81.2 0.0 copy-done
  81.3 3.6 %shard_map.62 = (f32[2,96]{1,0:T(2,128)S(1)}, f32[2,4608]{1,0:T(2,128)}) custom-call(bf16[128,5760]{1,0:T(8,128)(2,1)S(1)} %bitcast.28, f32[2,4608]{1,0:T(2,128)S(1)} %get-tuple-element.172, f32[1,4608]{1,0:T(1,128)S(1)} %reshape.73.gain, s32[4,128]{1,0:T(4,128)S(1)} %get-tuple-element.66.places, bf16[384,4608]{1,0:T(8,128)(2,1)S(1)} %copy-done), custom_call_target="tpu_custom_call" | custom-call | tf_op jit(solution)/shard_map/pallas_call | solution.py:244
  84.9 0.0 collective-permute-done.rows
  84.9 2.9 %shard_map.63 = f32[2,96]{1,0:T(2,128)S(1)} custom-call(bf16[128,5760]{1,0:T(8,128)(2,1)S(1)} %collective-permute-done.rows, f32[2,4608]{1,0:T(2,128)S(1)} %get-tuple-element.172, f32[1,4608]{1,0:T(1,128)S(1)} %reshape.73.gain, s32[4,128]{1,0:T(4,128)S(1)} %get-tuple-element.68.places, bf16[384,4608]{1,0:T(8,128)(2,1)S(1)} %copy-done), custom_call_target="tpu_custom_call" | custom-call | tf_op jit(solution)/shard_map/pallas_call | solution.py:244
  87.8 11.0 %all_to_all.38 = f32[32,2,96]{2,1,0:T(2,128)S(1)} all-to-all(f32[32,2,96]{2,1,0:T(2,128)S(1)} %bitcast.37), channel_id=1, replica_groups=mesh['dp_0'=4,'dp_1'=4,'dp_2'=2,'vocab'=16] {'dp_0','dp_1','dp_2'}, dimensions={0} | all-to-all | bytes 49152 | tf_op jit(solution)/shard_map/all_to_all | solution.py:25
  98.9 18.0 %all_to_all.39 = f32[16,2,96]{2,1,0:T(2,128)S(1)} all-to-all(f32[16,2,96]{2,1,0:T(2,128)S(1)} %broadcast_in_dim.30), channel_id=1, replica_groups=mesh['dp_0'=4,'dp_1'=4,'dp_2'=2,'vocab'=16] {'vocab'}, dimensions={0} | all-to-all | bytes 24576 | tf_op jit(solution)/shard_map/all_to_all | solution.py:25
  116.9 0.1 sub.20
  117.0 0.1 dynamic-slice_bitcast_fusion
  117.1 0.7 copy.24
  (21 shorter events, 0.3 us)
Async XLA Ops:
  0.6 25.2 %copy-start.2 = (s32[64,3]{0,1:T(4,128)S(1)}, s32[64,3]{0,1:T(4,128)}, u32[]{:S(2)}) copy-start(s32[64,3]{0,1:T(4,128)} %param.9) | copy-start | bytes 2308
  4.2 35.4 %copy-start.3 = (f32[4608]{0:T(1024)S(1)}, f32[4608]{0:T(1024)}, u32[]{:S(2)}) copy-start(f32[4608]{0:T(1024)} %param.7) | copy-start | bytes 55300
  4.2 48.9 %copy-start.1 = (f32[2,4608]{1,0:T(2,128)S(1)}, f32[2,4608]{1,0:T(2,128)}, u32[]{:S(2)}) copy-start(f32[2,4608]{1,0:T(2,128)} %own_hidden.3) | copy-start | bytes 110596
  4.2 20.3 %all-to-all-start.2 = ((bf16[32,4,1152]{2,1,0:T(4,128)(2,1)}), bf16[32,4,1152]{2,1,0:T(4,128)(2,1)S(1)}, u32[]{:S(2)}, u32[]{:S(2)}) async-start(bf16[32,4,1152]{2,1,0:T(4,128)(2,1)} %get-tuple-element.56), calls=%async_computation.2 | async-start | bytes 589824 | tf_op jit(solution)/shard_map/all_to_all | solution.py:25
  26.8 25.5 %all-to-all-start.3 = ((bf16[16,4,1152]{2,1,0:T(4,128)(2,1)}), bf16[16,4,1152]{2,1,0:T(4,128)(2,1)S(1)}, u32[]{:S(2)}, u32[]{:S(2)}) async-start(bf16[16,4,1152]{2,1,0:T(4,128)(2,1)} %shard_map.60), calls=%async_computation.3 | async-start | bytes 294912 | tf_op jit(solution)/shard_map/all_to_all | solution.py:25
  53.8 27.5 %copy-start = (bf16[384,4608]{1,0:T(8,128)(2,1)S(1)}, bf16[384,4608]{1,0:T(8,128)(2,1)}, u32[]{:S(2)}) copy-start(bf16[384,4608]{1,0:T(8,128)(2,1)} %get-tuple-element.171) | copy-start | bytes 10616836
  75.1 9.8 %collective-permute-start = (bf16[128,5760]{1,0:T(8,128)(2,1)S(1)}, bf16[128,5760]{1,0:T(8,128)(2,1)S(1)}, u32[]{:S(2)}, u32[]{:S(2)}) collective-permute-start(bf16[128,5760]{1,0:T(8,128)(2,1)S(1)} %bitcast.27), channel_id=1, source_target_pairs={{0,16},{16,0},{1,17},{17,1},{2,18},{18,2},{3,19},{19,3},{4,20},{20... | collective-permute-start | bytes 4423688 | tf_op jit(solution)/shard_map/ppermute | solution.py:33

commit v5 on v4

--- a/solution.py
+++ b/solution.py
@@ -15,6 +15,7 @@
 DP = ("dp_0", "dp_1", "dp_2")
 DP_VOCAB = ("dp_0", "dp_1", "dp_2", "vocab")
 PIECES = 4
+BLOCKS = 4
 SLOTS = 8
 
 epsilon_value = 1e-06
@@ -71,6 +72,20 @@
     width = row.shape[1] // PIECES
     parts = [placed(row[:, i * width : (i + 1) * width], i, PIECES) for i in range(PIECES)]
     return sum(parts[1:], parts[0])
+
+
+def pieces_of(block, index):
+    width = block.shape[1] // PIECES
+    to = lax.broadcasted_iota(jnp.int32, (2 * PIECES, block.shape[0]), 0)
+    of = lax.broadcasted_iota(jnp.int32, (2 * PIECES, block.shape[0]), 1)
+    total = jnp.zeros((2 * PIECES, width), jnp.float32)
+    for i in range(PIECES):
+        total = total + jnp.dot(
+            jnp.where((to == i) & (of == index), 1.0, 0.0).astype(jnp.bfloat16),
+            block[:, i * width : (i + 1) * width],
+            preferred_element_type=jnp.float32,
+        )
+    return total[:PIECES]
 
 
 def in_row(block):
@@ -92,78 +107,142 @@
     out[:, D:] = rest.astype(jnp.bfloat16)
 
 
-def lookup_kernel(
-    turn, tokens, tokens_again, hidden, table, rows, packed, rank_out, slots, held, found, sem
-):
+def token_keys(tokens, own_rows, shard_rows):
+    steps, summaries = tokens.shape
+    n_vocab = lax.axis_size("vocab")
+    summary = lax.broadcasted_iota(jnp.int32, tokens.shape, 1)
+    index = lax.broadcasted_iota(jnp.int32, tokens.shape, 0) * summaries + summary
+    holder = holder_of(tokens[...], shard_rows, lax.axis_size(DP) * n_vocab)
+    return holder, key_of(holder, index, summary, own_rows, n_vocab)
+
+
+def lookup_kernel(own_rows, turn, tokens, tokens_again, table, rows, held, found, sems):
     steps, summaries = tokens.shape
     shard_rows, n_groups, n_vocab = table.shape[0], rows.shape[0], lax.axis_size("vocab")
-    n_devices, own_rows = n_groups * n_vocab, hidden.shape[0]
-    lines, vocab = n_groups // 2, lax.axis_index("vocab")
+    lines, vocab, blocks = n_groups // 2, lax.axis_index("vocab"), held.shape[0]
     start = (lax.axis_index(DP) * n_vocab + vocab) * shard_rows
-    copy = pltpu.make_async_copy(table, held, sem)
-    copy.start()
+
+    def scan(summary, n):
+        for step in range(steps):
+            local = tokens[step, summary] - start
+            found[n] = step * summaries + summary
+            n = n + ((local >= 0) & (local < shard_rows)).astype(jnp.int32)
+        return n
+
+    n = lax.fori_loop(0, summaries, scan, jnp.int32(0))
+
+    def local_of(i):
+        step, summary = parted(found[i], summaries)
+        return tokens[step, summary] - start
+
+    def fetch(i, at):
+        first = pl.multiple_of(local_of(i) >> 4 << 4, 16)
+        return pltpu.make_async_copy(table.at[pl.ds(first, 16), :], held.at[at], sems.at[at])
+
+    def begin(first):
+        for at in range(blocks):
+
+            @pl.when(first + at < n)
+            def _():
+                fetch(first + at, at).start()
+
+    begin(jnp.int32(0))
     rows[...] = jnp.zeros_like(rows)
+    _, keys = token_keys(tokens_again, own_rows, shard_rows)
+
+    def give(i, at):
+        core = parted(parted(found[i], summaries)[1], own_rows)[0] & 1
+        key = ((core * n_vocab + vocab) << 8) + found[i]
+        before = keys < key
+        rank = jnp.sum(jnp.where(before, 1, 0)) - core * (steps * summaries // 2)
+        among = jnp.sum(jnp.where(before & ((keys ^ key) < 256), 1, 0))
+        fetch(i, at).wait()
+
+        @pl.when(parted(among, lines)[0] == turn[0])
+        def _():
+            row = pieces_of(held[at], local_of(i) & 15)
+            rows[parted(rank, lines)[1] * 2 + core] = row.astype(jnp.bfloat16)
+
+    def several(i, _):
+        first = i * blocks
+        pl.when(i > 0)(lambda: begin(first))
+        for at in range(blocks):
+            pl.when(first + at < n)(functools.partial(give, first + at, at))
+        return 0
+
+    lax.fori_loop(0, (n + blocks - 1) // blocks, several, 0)
+
+
+def plan_kernel(shard_rows, tokens, hidden, packed, mine, theirs, slots):
+    steps, summaries = tokens.shape
+    own_rows, lines = hidden.shape[0], lax.axis_size(XY)
     split(hidden, packed)
-    summary_of = lax.broadcasted_iota(jnp.int32, tokens.shape, 1)
-    index_of = lax.broadcasted_iota(jnp.int32, tokens.shape, 0) * summaries + summary_of
-    holders = holder_of(tokens_again[...], shard_rows, n_devices)
-    keys = key_of(holders, index_of, summary_of, own_rows, n_vocab)
-
-    def scan(summary, state):
-        n, rank, among = state
-        for step in range(steps):
-            token, index = tokens[step, summary], step * summaries + summary
-            local = token - start
-            found[n] = index
-            n = n + ((local >= 0) & (local < shard_rows)).astype(jnp.int32)
-            holder = holder_of(token, shard_rows, n_devices)
-            key = key_of(holder, index, summary, own_rows, n_vocab)
-            before = key < keys
-            rank = rank + jnp.where(before, 1, 0)
-            among = among + jnp.where(before & ((key ^ keys) < 256), 1, 0)
-        return n, rank, among
-
-    none = jnp.zeros(tokens.shape, jnp.int32)
-    n, rank, among = lax.fori_loop(0, summaries, scan, (jnp.int32(0), none, none))
-    rank_out[...] = rank
-    turns = parted(among, lines)[0]
-    first = lax.axis_index("dp_2") * (steps * summaries // 2) + lax.axis_index(XY)
+    holders, keys = token_keys(tokens, own_rows, shard_rows)
+    upright = jnp.transpose(keys)
+    rank, among = [], []
+    for step in range(steps):
+        key = keys[step : step + 1, :]
+        before = [upright[:, i : i + 1] < key for i in range(steps)]
+        near = [(upright[:, i : i + 1] ^ key) < 256 for i in range(steps)]
+        counts = sum(jnp.where(x, 1, 0) for x in before)
+        rank.append(jnp.sum(counts, axis=0, keepdims=True))
+        counts = sum(jnp.where(x & y, 1, 0) for x, y in zip(before, near))
+        among.append(jnp.sum(counts, axis=0, keepdims=True))
+    rank, among = jnp.concatenate(rank, axis=0), jnp.concatenate(among, axis=0)
+    turns, core, per_half = parted(among, lines)[0], lax.axis_index("dp_2"), rank.size // 2
     for i in range(slots.shape[1]):
-        hit = rank == first + i * lines
+        hit = rank == core * per_half + lax.axis_index(XY) + i * lines
         slots[0, i] = jnp.sum(jnp.where(hit, holders, 0))
         slots[1, i] = jnp.sum(jnp.where(hit, turns, 0))
         slots[2, i] = jnp.int32(0)
     slots[2, 0] = jnp.max(turns) + 1
-    copy.wait()
-
-    def give(i, _):
-        index = found[i]
-        step, summary = parted(index, summaries)
-        local = tokens[step, summary] - start
-        core = parted(summary, own_rows)[0] & 1
-        at = index_of == index
-        its_rank = jnp.sum(jnp.where(at, rank, 0)) - core * (steps * summaries // 2)
-        its_turn = jnp.sum(jnp.where(at, turns, 0))
-
-        @pl.when(its_turn == turn[0])
-        def _():
-            block = held[pl.ds(pl.multiple_of(local // 16 * 16, 16), 16), :]
-            row = in_pieces(picked(block, local % 16))
-            rows[parted(its_rank, lines)[1] * 2 + core] = row.astype(jnp.bfloat16)
-
-        return 0
-
-    lax.fori_loop(0, n, give, 0)
+
+    slot, line = parted(jnp.where(rank < per_half, rank, rank - per_half), lines)
+    start = (
+        lax.axis_index(DP) * lax.axis_size("vocab") + lax.axis_index("vocab")
+    ) * shard_rows
+    local = tokens[...] - start
+    entry = jnp.where((local >= 0) & (local < shard_rows), local + 1, 0)
+    wide = mine.shape[1]
+    source = lax.broadcasted_iota(jnp.int32, (summaries, wide), 0)
+    lane = lax.broadcasted_iota(jnp.int32, (summaries, wide), 1)
+    lanes = lax.broadcasted_iota(jnp.int32, (1, wide), 1)
+
+    def chosen(values, summary, block):
+        taken = jnp.dot(
+            values.astype(jnp.float32),
+            jnp.where(source == summary, 1.0, 0.0),
+            preferred_element_type=jnp.float32,
+        )
+        at = [jnp.where(parted(lanes, block)[0] == i, taken[i : i + 1], 0.0) for i in range(steps)]
+        return sum(at).astype(jnp.int32)
+
+    half = summaries // 2
+    own = lax.axis_index(DP) * own_rows + parted(lane, own_rows)[1]
+    for out, its_core in ((mine, core), (theirs, 1 - core)):
+        chip, row = parted(parted(lane, half)[1], own_rows)
+        summary = (chip * 2 + its_core) * own_rows + row
+        high, low = (chosen(x, summary, half) for x in (entry >> 4, entry & 15))
+        place = line * SLOTS + slot
+        out[...] = jnp.concatenate(
+            [
+                chosen(place, summary, half),
+                (high << 4) + low - 1,
+                chosen(place, own, own_rows),
+                jnp.zeros((1, wide), jnp.int32),
+            ],
+            axis=0,
+        )
 
 
 def relay_kernel(turn, slots, rows, out, buffer, sem):
-    n_vocab = out.shape[0]
     out[...] = jnp.zeros_like(out)
     for i in range(slots.shape[1]):
-
-        @pl.when((slots[0, i] % n_vocab == lax.axis_index("vocab")) & (slots[1, i] == turn[0]))
+        source, plane = parted(slots[0, i], out.shape[0])
+
+        @pl.when((plane == lax.axis_index("vocab")) & (slots[1, i] == turn[0]))
         def _():
-            copy = pltpu.make_async_copy(rows.at[slots[0, i] // n_vocab], buffer, sem)
+            copy = pltpu.make_async_copy(rows.at[source], buffer, sem)
             copy.start()
             copy.wait()
             out[...] = jnp.broadcast_to(buffer[...][None], out.shape)
@@ -172,7 +251,7 @@
 def pack_kernel(turn, slots, rows, before, out):
     total = before[:, :D].astype(jnp.float32)
     for i in range(slots.shape[1]):
-        row = in_row(rows[slots[0, i] % rows.shape[0]])
+        row = in_row(rows[parted(slots[0, i], rows.shape[0])[1]])
         total = total + placed(row, jnp.where(slots[1, i] == turn[0], i, -1), out.shape[0])
     out[:, :D] = total.astype(jnp.bfloat16)
     out[:, D:] = before[:, D:]
@@ -181,9 +260,10 @@
 def head_kernel(rows, own_hidden, gain, places, table, out, *more):
     *final, gain_in, places_in, held, normed, sems = more
     final = final[0] if final else None
+    pairs = [(places, places_in), (gain, gain_in), (table, held)]
     copies = [
         pltpu.make_async_copy(x, y, sems.at[i])
-        for i, (x, y) in enumerate([(places, places_in), (gain, gain_in), (table, held)])
+        for i, (x, y) in enumerate(pairs if final is not None else pairs[:2])
     ]
     for copy in copies:
         copy.start()
@@ -220,9 +300,10 @@
         normed[pl.ds(step * count, count), :] = state.astype(jnp.bfloat16)
         if step < steps - 1:
             current = current + math.sqrt(D) * looked[step * count : (step + 1) * count]
-    copies[2].wait()
+    for copy in copies[2:]:
+        copy.wait()
     logits = lax.dot_general(
-        held[...], normed[...], (((1,), (1,)), ((), ())), preferred_element_type=jnp.float32
+        (held if copies[2:] else table)[...], normed[...], (((1,), (1,)), ((), ())), preferred_element_type=jnp.float32
     )
     capped = softcap_value * jnp.tanh(logits / softcap_value)
     exp_total = jnp.sum(jnp.exp(capped), axis=0, keepdims=True)
@@ -239,17 +320,18 @@
     final[...] = current
 
 
-def on_chip(kernel, out_shape, scratch, *operands):
+def on_chip(kernel, out_shape, scratch, *operands, scalars=None, cost=None):
     operands = [x if isinstance(x, tuple) else (x, pltpu.VMEM) for x in operands]
     return pl.pallas_call(
         kernel,
         out_shape=out_shape,
         in_specs=[pl.BlockSpec(memory_space=space) for _, space in operands],
         out_specs=jax.tree.map(
-            lambda x: pl.BlockSpec(memory_space=pltpu.SMEM if x.shape[0] == 3 and x.shape[1] < SLOTS else pltpu.VMEM),
+            lambda x: pl.BlockSpec(memory_space=pltpu.SMEM if x is scalars else pltpu.VMEM),
             out_shape,
         ),
         scratch_shapes=scratch,
+        cost_estimate=cost,
         compiler_params=pltpu.CompilerParams(vmem_limit_bytes=24 * 2**20),
     )(*(x for x, _ in operands))
 
@@ -259,7 +341,6 @@
     shard_rows = embed_table.shape[0]
     n_xy, n_groups, n_vocab = lax.axis_size(XY), lax.axis_size(DP), lax.axis_size("vocab")
     chip, core, summaries = lax.axis_index(XY), lax.axis_index("dp_2"), tokens.shape[0]
-    start = (lax.axis_index(DP) * n_vocab + lax.axis_index("vocab")) * shard_rows
     half = summaries // 2
     bf16, f32, i32 = jnp.bfloat16, jnp.float32, jnp.int32
     by_step = jnp.transpose(tokens)
@@ -270,29 +351,45 @@
 
     def lookup(turn):
         return on_chip(
-            lookup_kernel,
-            (
-                jax.ShapeDtypeStruct((n_groups, *row_shape), bf16),
-                jax.ShapeDtypeStruct((SLOTS, D + D // PIECES), bf16),
-                jax.ShapeDtypeStruct(by_step.shape, i32),
-                jax.ShapeDtypeStruct((3, n_slots), i32),
-            ),
+            functools.partial(lookup_kernel, own_rows),
+            jax.ShapeDtypeStruct((n_groups, *row_shape), bf16),
             [
-                pltpu.VMEM(embed_table.shape, bf16),
+                pltpu.VMEM((BLOCKS, 16, D), bf16),
                 pltpu.SMEM((STEPS * summaries + 1,), i32),
-                pltpu.SemaphoreType.DMA,
+                pltpu.SemaphoreType.DMA((BLOCKS,)),
             ],
             (turn, pltpu.SMEM),
             (by_step, pltpu.SMEM),
             by_step,
-            hidden,
             (embed_table, pl.ANY),
         )
 
     first = jnp.zeros((1,), i32)
-    rows, packed, rank, slots = lookup(first)
+    rows, shared, all_tokens, gain = lax.optimization_barrier(
+        (lookup(first), hidden, by_step, norm_gain)
+    )
+    rows = exchange(rows, DP)
+    wide = n_xy * SLOTS
+    slots = jax.ShapeDtypeStruct((3, n_slots), i32)
+    packed, places_mine, places_theirs, slots = on_chip(
+        functools.partial(plan_kernel, shard_rows),
+        (
+            jax.ShapeDtypeStruct((SLOTS, D + D // PIECES), bf16),
+            jax.ShapeDtypeStruct((4, wide), i32),
+            jax.ShapeDtypeStruct((4, wide), i32),
+            slots,
+        ),
+        [],
+        all_tokens,
+        shared,
+        scalars=slots,
+        cost=pl.CostEstimate(flops=0, bytes_accessed=2**23, transcendentals=0),
+    )
+    gain = gain.reshape(1, D)
     turns = slots[2, 0]
-    rows = exchange(rows, DP)
+    rows, packed, places_mine, places_theirs, slots, turns, gain = lax.optimization_barrier(
+        (rows, packed, places_mine, places_theirs, slots, turns, gain)
+    )
 
     def relay(turn, rows):
         return on_chip(
@@ -315,42 +412,18 @@
             packed,
         )
 
-    rows = relay(first, rows)
-    rows, rank, flat, gain = lax.optimization_barrier((rows, rank, by_step, norm_gain))
-    rows = exchange(rows, "vocab")
-    gain = gain.reshape(1, D)
-
-    def halves(x):
-        x = jnp.transpose(x.reshape(STEPS, n_xy, 2, own_rows), (2, 0, 1, 3)).reshape(2, per_half)
-        return jnp.where(core == 0, x, x[::-1])
-
-    place = rank - jnp.where(rank < per_half, 0, per_half)
-    slot, line = parted(place, n_xy)
-    place = halves(line * SLOTS + slot)
-    own = lax.dynamic_slice_in_dim(
-        place[0].reshape(STEPS, half), chip * own_rows, own_rows, 1
-    ).reshape(1, STEPS * own_rows)
-    wide = n_xy * SLOTS
-
-    def widened(x):
-        return jnp.pad(x, ((0, 0), (0, wide - x.shape[1])), constant_values=-1)
-
-    own = widened(jnp.concatenate([own, own]).reshape(2, -1)[:, : STEPS * own_rows])
-    places = jnp.stack(
-        [widened(place[:, : 2 * half]), widened(halves(flat - start)), own, own], axis=1
-    )
-    places_mine, places_theirs = places[0], places[1]
-    rows, places_mine, places_theirs, gain = lax.optimization_barrier(
-        (rows, places_mine, places_theirs, gain)
-    )
+    rows = exchange(relay(first, rows), "vocab")
 
     def further(state):
         turn = state[0][None]
-        rows = exchange(relay(turn, exchange(lookup(turn)[0], DP)), "vocab")
+        rows = exchange(relay(turn, exchange(lookup(turn), DP)), "vocab")
         return state[0] + 1, pack(turn, rows, state[1])
 
-    _, packed = lax.while_loop(
-        lambda state: state[0] < turns, further, (jnp.int32(1), pack(first, rows, packed))
+    packed = lax.cond(
+        turns > 1,
+        lambda x: lax.while_loop(lambda state: state[0] < turns, further, (jnp.int32(1), x))[1],
+        lambda x: x,
+        pack(first, rows, packed),
     )
     of_mine = to_each(packed, XY).reshape(wide, D + D // PIECES)
     of_theirs = other_core(of_mine)
@@ -362,7 +435,7 @@
             [
                 pltpu.VMEM((1, D), f32),
                 pltpu.VMEM(places.shape, i32),
-                pltpu.VMEM(embed_table.shape, bf16),
+                pltpu.VMEM(embed_table.shape if more else (16, 128), bf16),
                 pltpu.VMEM((per_half, D), bf16),
                 pltpu.SemaphoreType.DMA((3,)),
             ],
@@ -370,7 +443,7 @@
             hidden,
             (gain, pl.ANY),
             (places, pl.ANY),
-            (embed_table, pl.ANY),
+            (embed_table, pl.ANY if more else pltpu.VMEM),
         )
 
     for_mine, final_hidden = totals(

time: 118 us -> 117 us (level)
  blocking collectives: 50.2 us -> 31 us
  waiting for transfers between devices: 21.4 us -> 31.2 us
  starting transfers between devices: 29.7 us -> 38.5 us
    all_to_all x3 -> x2, blocking collectives: 50.2 us -> 31 us  [exchange(): return lax.all_to_all(x, axis, split_axis=0, concat_axis=0, tiled=True)]
    all_to_all x2 -> x3, waiting for transfers between devices: 21.4 us -> 31.1 us  [exchange(): return lax.all_to_all(x, axis, split_axis=0, concat_axis=0, tiled=True)]
    all_to_all x2 -> x3, starting transfers between devices: 23.6 us -> 31.4 us  [exchange(): return lax.all_to_all(x, axis, split_axis=0, concat_axis=0, tiled=True)]
    pallas_call x5 -> x6, Pallas kernels: 12.3 us -> 12.3 us  [on_chip(): pl.pallas_call(kernel, out_shape=out_shape, in_specs=[pl.BlockSpec(memory...]
  transfers between devices with their start and end apart: 3 -> 4, of which waited for: 2 -> 3; matrix products, arithmetic and copies ran while one was open for 1% -> 0% of each run, Pallas kernels for 3% -> 4%
where the time goes in v5:
time: 117 us
  starting transfers between devices  38.5 us (33%)
  waiting for transfers between devices  31.2 us (27%)
  blocking collectives  31 us (26%)
  Pallas kernels  12.3 us (11%)
  local copies, waits for them, and re-layouts  2.07 us (2%)
  between operations  1.48 us (1%)
    all_to_all x3, starting transfers between devices, exchange(): return lax.all_to_all(x, axis, split_axis=0, concat_axis=0, tiled=True)  31.4 us
    all_to_all x3, waiting for transfers between devices, exchange(): return lax.all_to_all(x, axis, split_axis=0, concat_axis=0, tiled=True)  31.1 us
    all_to_all x2, blocking collectives, exchange(): return lax.all_to_all(x, axis, split_axis=0, concat_axis=0, tiled=True)  31 us
    pallas_call x6, Pallas kernels, on_chip(): pl.pallas_call(kernel, out_shape=out_shape, in_specs=[pl.BlockSpec(memory...  12.3 us
    ppermute x1, starting transfers between devices, other_core(): return lax.ppermute(x, 'dp_2', [(0, 1), (1, 0)])  7.12 us
  transfers between devices with their start and end apart: 4, of which 3 were waited for; matrix products, arithmetic and copies ran while one was open for 0% of the time, Pallas kernels for 4%

profile of v5, /device:TPU:1, one launch (start us, length us, event | category | flops | bytes accessed | tf_op | source)
XLA Modules:
  0.0 116.6 jit_solution(1773695607634913104)
XLA Ops:
  0.6 0.0 copy-start
  0.6 0.0 copy-start.2
  0.6 0.0 copy-start.3
  0.7 2.6 %shard_map.59 = bf16[32,4,1152]{2,1,0:T(4,128)(2,1)} custom-call(s32[1]{0:T(128)} %constant.11.clone.1.turn, s32[3,64]{1,0:T(4,128)} %bitcast.15, s32[3,64]{1,0:T(4,128)} %bitcast.16, bf16[384,4608]{1,0:T(8,128)(2,1)} %table.5), custom_call_target="tpu_custom_call" | custom-call | tf_op jit(solution)/shard_map/pallas_call | solution.py:325
  3.3 11.5 %all-to-all-start.2 = ((bf16[32,4,1152]{2,1,0:T(4,128)(2,1)}), bf16[32,4,1152]{2,1,0:T(4,128)(2,1)S(1)}, u32[]{:S(2)}, u32[]{:S(2)}) async-start(bf16[32,4,1152]{2,1,0:T(4,128)(2,1)} %shard_map.59), calls=%async_computation.2 | async-start | bytes 589824 | tf_op jit(solution)/shard_map/all_to_all | solution.py:26
  14.8 0.0 copy-done
  14.8 0.0 copy-done.2
  14.8 1.1 shard_map.60
  15.9 0.5 slice.9
  16.4 0.0 copy-done.3
  16.4 7.8 %all-to-all-done.2.rows = bf16[32,4,1152]{2,1,0:T(4,128)(2,1)S(1)} async-done(((bf16[32,4,1152]{2,1,0:T(4,128)(2,1)}), bf16[32,4,1152]{2,1,0:T(4,128)(2,1)S(1)}, u32[]{:S(2)}, u32[]{:S(2)}) %all-to-all-start.2) | async-done | bytes 294944 | tf_op jit(solution)/shard_map/all_to_all | solution.py:26
  24.2 1.3 %shard_map.61 = bf16[16,4,1152]{2,1,0:T(4,128)(2,1)} custom-call(s32[1]{0:T(128)} %constant.11.clone.1.turn, s32[3,6]{1,0:T(4,128)S(1)} %get-tuple-element.80.slots, bf16[32,4,1152]{2,1,0:T(4,128)(2,1)S(1)} %all-to-all-done.2.rows), custom_call_target="tpu_custom_call" | custom-call | tf_op jit(solution)/shard_map/pallas_call | solution.py:325
  25.5 13.1 %all-to-all-start.3 = ((bf16[16,4,1152]{2,1,0:T(4,128)(2,1)}), bf16[16,4,1152]{2,1,0:T(4,128)(2,1)S(1)}, u32[]{:S(2)}, u32[]{:S(2)}) async-start(bf16[16,4,1152]{2,1,0:T(4,128)(2,1)} %shard_map.61), calls=%async_computation.3 | async-start | bytes 294912 | tf_op jit(solution)/shard_map/all_to_all | solution.py:26
  39.3 12.0 %all-to-all-done.3.rows = bf16[16,4,1152]{2,1,0:T(4,128)(2,1)S(1)} async-done(((bf16[16,4,1152]{2,1,0:T(4,128)(2,1)}), bf16[16,4,1152]{2,1,0:T(4,128)(2,1)S(1)}, u32[]{:S(2)}, u32[]{:S(2)}) %all-to-all-start.3) | async-done | bytes 147488 | tf_op jit(solution)/shard_map/all_to_all | solution.py:26
  51.3 0.9 shard_map.62
  52.2 0.1 broadcast_in_dim.9
  52.3 20.0 %all_to_all.37 = bf16[16,8,5760]{2,1,0:T(8,128)(2,1)S(1)} all-to-all(bf16[16,8,5760]{2,1,0:T(8,128)(2,1)S(1)} %broadcast_in_dim.9), channel_id=1, replica_groups=mesh['dp_0'=4,'dp_1'=4,'dp_2'=2,'vocab'=16] {'dp_0','dp_1'}, dimensions={0} | all-to-all | bytes 2949120 | tf_op jit(solution)/shard_map/all_to_all | solution.py:26
  72.3 7.1 %collective-permute-start = (bf16[128,5760]{1,0:T(8,128)(2,1)S(1)}, bf16[128,5760]{1,0:T(8,128)(2,1)S(1)}, u32[]{:S(2)}, u32[]{:S(2)}) collective-permute-start(bf16[128,5760]{1,0:T(8,128)(2,1)S(1)} %bitcast.11), channel_id=1, source_target_pairs={{0,16},{16,0},{1,17},{17,1},{2,18},{18,2},{3,19},{19,3},{4,20},{20... | collective-permute-start | bytes 4423688 | tf_op jit(solution)/shard_map/ppermute | solution.py:34
  79.4 0.0 copy-start.1
  79.4 4.1 %shard_map.63 = (f32[2,96]{1,0:T(2,128)S(1)}, f32[2,4608]{1,0:T(2,128)}) custom-call(bf16[128,5760]{1,0:T(8,128)(2,1)S(1)} %bitcast.12, f32[2,4608]{1,0:T(2,128)S(1)} %copy-done, f32[1,4608]{1,0:T(1,128)S(1)} %reshape.53.gain, s32[4,128]{1,0:T(4,128)S(1)} %get-tuple-element.84.places, bf16[384,4608]{1,0:T(8,128)(2,1)} %table.5), custom_call_target="tpu_custom_call" | custom-call | tf_op jit(solution)/shard_map/pallas_call | solution.py:325
  83.6 0.0 collective-permute-done.rows
  83.6 0.0 copy-done.1
  83.6 2.3 %shard_map.64 = f32[2,96]{1,0:T(2,128)S(1)} custom-call(bf16[128,5760]{1,0:T(8,128)(2,1)S(1)} %collective-permute-done.rows, f32[2,4608]{1,0:T(2,128)S(1)} %copy-done, f32[1,4608]{1,0:T(1,128)S(1)} %reshape.53.gain, s32[4,128]{1,0:T(4,128)S(1)} %get-tuple-element.86.places, bf16[384,4608]{1,0:T(8,128)(2,1)S(1)} %copy-done.1), custom_call_target="tpu_custom_call" | custom-call | tf_op jit(solution)/shard_map/pallas_call | solution.py:325
  85.9 11.0 %all_to_all.38 = f32[32,2,96]{2,1,0:T(2,128)S(1)} all-to-all(f32[32,2,96]{2,1,0:T(2,128)S(1)} %bitcast.19), channel_id=1, replica_groups=mesh['dp_0'=4,'dp_1'=4,'dp_2'=2,'vocab'=16] {'dp_0','dp_1','dp_2'}, dimensions={0} | all-to-all | bytes 49152 | tf_op jit(solution)/shard_map/all_to_all | solution.py:26
  97.0 0.6 broadcast_in_dim.11
  97.6 6.8 %all-to-all-start.6 = ((f32[16,2,96]{2,1,0:T(2,128)}), f32[16,2,96]{2,1,0:T(2,128)S(1)}, u32[]{:S(2)}, u32[]{:S(2)}) async-start(f32[16,2,96]{2,1,0:T(2,128)} %broadcast_in_dim.11), calls=%async_computation.6 | async-start | bytes 32768 | tf_op jit(solution)/shard_map/all_to_all | solution.py:26
  104.4 11.4 %all-to-all-done.6 = f32[16,2,96]{2,1,0:T(2,128)S(1)} async-done(((f32[16,2,96]{2,1,0:T(2,128)}), f32[16,2,96]{2,1,0:T(2,128)S(1)}, u32[]{:S(2)}, u32[]{:S(2)}) %all-to-all-start.6) | async-done | bytes 12320 | tf_op jit(solution)/shard_map/all_to_all | solution.py:26
  115.8 0.1 sub.8
  115.9 0.1 dynamic-slice_bitcast_fusion
  116.0 0.7 copy.11
  (7 shorter events, 0.1 us)
Async XLA Ops:
  0.6 14.1 %copy-start = (f32[2,4608]{1,0:T(2,128)S(1)}, f32[2,4608]{1,0:T(2,128)}, u32[]{:S(2)}) copy-start(f32[2,4608]{1,0:T(2,128)} %own_hidden.3) | copy-start | bytes 110596
  0.6 14.1 %copy-start.2 = (s32[64,3]{0,1:T(4,128)S(1)}, s32[64,3]{0,1:T(4,128)}, u32[]{:S(2)}) copy-start(s32[64,3]{0,1:T(4,128)} %param.11) | copy-start | bytes 2308
  0.6 15.7 %copy-start.3 = (f32[4608]{0:T(1024)S(1)}, f32[4608]{0:T(1024)}, u32[]{:S(2)}) copy-start(f32[4608]{0:T(1024)} %param.9) | copy-start | bytes 55300
  3.3 20.9 %all-to-all-start.2 = ((bf16[32,4,1152]{2,1,0:T(4,128)(2,1)}), bf16[32,4,1152]{2,1,0:T(4,128)(2,1)S(1)}, u32[]{:S(2)}, u32[]{:S(2)}) async-start(bf16[32,4,1152]{2,1,0:T(4,128)(2,1)} %shard_map.59), calls=%async_computation.2 | async-start | bytes 589824 | tf_op jit(solution)/shard_map/all_to_all | solution.py:26
  25.5 25.8 %all-to-all-start.3 = ((bf16[16,4,1152]{2,1,0:T(4,128)(2,1)}), bf16[16,4,1152]{2,1,0:T(4,128)(2,1)S(1)}, u32[]{:S(2)}, u32[]{:S(2)}) async-start(bf16[16,4,1152]{2,1,0:T(4,128)(2,1)} %shard_map.61), calls=%async_computation.3 | async-start | bytes 294912 | tf_op jit(solution)/shard_map/all_to_all | solution.py:26
  72.3 11.3 %collective-permute-start = (bf16[128,5760]{1,0:T(8,128)(2,1)S(1)}, bf16[128,5760]{1,0:T(8,128)(2,1)S(1)}, u32[]{:S(2)}, u32[]{:S(2)}) collective-permute-start(bf16[128,5760]{1,0:T(8,128)(2,1)S(1)} %bitcast.11), channel_id=1, source_target_pairs={{0,16},{16,0},{1,17},{17,1},{2,18},{18,2},{3,19},{19,3},{4,20},{20... | collective-permute-start | bytes 4423688 | tf_op jit(solution)/shard_map/ppermute | solution.py:34
  79.4 4.2 %copy-start.1 = (bf16[384,4608]{1,0:T(8,128)(2,1)S(1)}, bf16[384,4608]{1,0:T(8,128)(2,1)}, u32[]{:S(2)}) copy-start(bf16[384,4608]{1,0:T(8,128)(2,1)} %table.5) | copy-start | bytes 10616836
  97.6 18.2 %all-to-all-start.6 = ((f32[16,2,96]{2,1,0:T(2,128)}), f32[16,2,96]{2,1,0:T(2,128)S(1)}, u32[]{:S(2)}, u32[]{:S(2)}) async-start(f32[16,2,96]{2,1,0:T(2,128)} %broadcast_in_dim.11), calls=%async_computation.6 | async-start | bytes 32768 | tf_op jit(solution)/shard_map/all_to_all | solution.py:26

commit v6 on v5

--- a/solution.py
+++ b/solution.py
@@ -235,17 +235,14 @@
         )
 
 
-def relay_kernel(turn, slots, rows, out, buffer, sem):
+def relay_kernel(turn, slots, rows, out):
     out[...] = jnp.zeros_like(out)
     for i in range(slots.shape[1]):
         source, plane = parted(slots[0, i], out.shape[0])
 
         @pl.when((plane == lax.axis_index("vocab")) & (slots[1, i] == turn[0]))
         def _():
-            copy = pltpu.make_async_copy(rows.at[source], buffer, sem)
-            copy.start()
-            copy.wait()
-            out[...] = jnp.broadcast_to(buffer[...][None], out.shape)
+            out[...] = jnp.broadcast_to(rows[source][None], out.shape)
 
 
 def pack_kernel(turn, slots, rows, before, out):
@@ -395,10 +392,10 @@
         return on_chip(
             relay_kernel,
             jax.ShapeDtypeStruct((n_vocab, *row_shape), bf16),
-            [pltpu.VMEM(row_shape, bf16), pltpu.SemaphoreType.DMA],
+            [],
             (turn, pltpu.SMEM),
             (slots, pltpu.SMEM),
-            (rows, pl.ANY),
+            rows,
         )
 
     def pack(turn, rows, packed):

time: 117 us -> 117 us (level)
  no operation moved by 1% of the time
where the time goes in v6:
time: 117 us; the launch traced here: 116 us
  starting transfers between devices  38.2 us (33%)
  blocking collectives  31.2 us (27%)
  waiting for transfers between devices  31 us (26%)
  Pallas kernels  12.3 us (11%)
  local copies, waits for them, and re-layouts  2.07 us (2%)
  between operations  1.47 us (1%)
    all_to_all x2, blocking collectives, exchange(): return lax.all_to_all(x, axis, split_axis=0, concat_axis=0, tiled=True)  31.2 us
    all_to_all x3, starting transfers between devices, exchange(): return lax.all_to_all(x, axis, split_axis=0, concat_axis=0, tiled=True)  31 us
    all_to_all x3, waiting for transfers between devices, exchange(): return lax.all_to_all(x, axis, split_axis=0, concat_axis=0, tiled=True)  31 us
    pallas_call x6, Pallas kernels, on_chip(): pl.pallas_call(kernel, out_shape=out_shape, in_specs=[pl.BlockSpec(memory...  12.3 us
    ppermute x1, starting transfers between devices, other_core(): return lax.ppermute(x, 'dp_2', [(0, 1), (1, 0)])  7.12 us
  transfers between devices with their start and end apart: 4, of which 3 were waited for; matrix products, arithmetic and copies ran while one was open for 0% of the time, Pallas kernels for 4%

profile of v6, /device:TPU:1, one launch (start us, length us, event | category | flops | bytes accessed | tf_op | source)
XLA Modules:
  0.0 116.3 jit_solution(18423620278836575605)
XLA Ops:
  0.6 0.0 copy-start
  0.6 0.0 copy-start.2
  0.6 0.0 copy-start.3
  0.7 2.6 %shard_map.59 = bf16[32,4,1152]{2,1,0:T(4,128)(2,1)} custom-call(s32[1]{0:T(128)} %constant.11.clone.1.turn, s32[3,64]{1,0:T(4,128)} %bitcast.15, s32[3,64]{1,0:T(4,128)} %bitcast.16, bf16[384,4608]{1,0:T(8,128)(2,1)} %table.5), custom_call_target="tpu_custom_call" | custom-call | tf_op jit(solution)/shard_map/pallas_call | solution.py:322
  3.3 11.5 %all-to-all-start.2 = ((bf16[32,4,1152]{2,1,0:T(4,128)(2,1)}), bf16[32,4,1152]{2,1,0:T(4,128)(2,1)S(1)}, u32[]{:S(2)}, u32[]{:S(2)}) async-start(bf16[32,4,1152]{2,1,0:T(4,128)(2,1)} %shard_map.59), calls=%async_computation.2 | async-start | bytes 589824 | tf_op jit(solution)/shard_map/all_to_all | solution.py:26
  14.8 0.0 copy-done
  14.8 0.0 copy-done.2
  14.8 1.1 shard_map.60
  15.9 0.5 slice.9
  16.4 0.0 copy-done.3
  16.4 7.8 %all-to-all-done.2.rows = bf16[32,4,1152]{2,1,0:T(4,128)(2,1)S(1)} async-done(((bf16[32,4,1152]{2,1,0:T(4,128)(2,1)}), bf16[32,4,1152]{2,1,0:T(4,128)(2,1)S(1)}, u32[]{:S(2)}, u32[]{:S(2)}) %all-to-all-start.2) | async-done | bytes 294944 | tf_op jit(solution)/shard_map/all_to_all | solution.py:26
  24.2 1.3 %shard_map.61 = bf16[16,4,1152]{2,1,0:T(4,128)(2,1)} custom-call(s32[1]{0:T(128)} %constant.11.clone.1.turn, s32[3,6]{1,0:T(4,128)S(1)} %get-tuple-element.80.slots, bf16[32,4,1152]{2,1,0:T(4,128)(2,1)S(1)} %all-to-all-done.2.rows), custom_call_target="tpu_custom_call" | custom-call | tf_op jit(solution)/shard_map/pallas_call | solution.py:322
  25.5 12.8 %all-to-all-start.3 = ((bf16[16,4,1152]{2,1,0:T(4,128)(2,1)}), bf16[16,4,1152]{2,1,0:T(4,128)(2,1)S(1)}, u32[]{:S(2)}, u32[]{:S(2)}) async-start(bf16[16,4,1152]{2,1,0:T(4,128)(2,1)} %shard_map.61), calls=%async_computation.3 | async-start | bytes 294912 | tf_op jit(solution)/shard_map/all_to_all | solution.py:26
  38.9 11.8 %all-to-all-done.3.rows = bf16[16,4,1152]{2,1,0:T(4,128)(2,1)S(1)} async-done(((bf16[16,4,1152]{2,1,0:T(4,128)(2,1)}), bf16[16,4,1152]{2,1,0:T(4,128)(2,1)S(1)}, u32[]{:S(2)}, u32[]{:S(2)}) %all-to-all-start.3) | async-done | bytes 147488 | tf_op jit(solution)/shard_map/all_to_all | solution.py:26
  50.8 0.9 shard_map.62
  51.7 0.1 broadcast_in_dim.9
  51.8 20.1 %all_to_all.37 = bf16[16,8,5760]{2,1,0:T(8,128)(2,1)S(1)} all-to-all(bf16[16,8,5760]{2,1,0:T(8,128)(2,1)S(1)} %broadcast_in_dim.9), channel_id=1, replica_groups=mesh['dp_0'=4,'dp_1'=4,'dp_2'=2,'vocab'=16] {'dp_0','dp_1'}, dimensions={0} | all-to-all | bytes 2949120 | tf_op jit(solution)/shard_map/all_to_all | solution.py:26
  72.0 7.1 %collective-permute-start = (bf16[128,5760]{1,0:T(8,128)(2,1)S(1)}, bf16[128,5760]{1,0:T(8,128)(2,1)S(1)}, u32[]{:S(2)}, u32[]{:S(2)}) collective-permute-start(bf16[128,5760]{1,0:T(8,128)(2,1)S(1)} %bitcast.11), channel_id=1, source_target_pairs={{0,16},{16,0},{1,17},{17,1},{2,18},{18,2},{3,19},{19,3},{4,20},{20... | collective-permute-start | bytes 4423688 | tf_op jit(solution)/shard_map/ppermute | solution.py:34
  79.1 0.0 copy-start.1
  79.1 4.1 %shard_map.63 = (f32[2,96]{1,0:T(2,128)S(1)}, f32[2,4608]{1,0:T(2,128)}) custom-call(bf16[128,5760]{1,0:T(8,128)(2,1)S(1)} %bitcast.12, f32[2,4608]{1,0:T(2,128)S(1)} %copy-done, f32[1,4608]{1,0:T(1,128)S(1)} %reshape.53.gain, s32[4,128]{1,0:T(4,128)S(1)} %get-tuple-element.84.places, bf16[384,4608]{1,0:T(8,128)(2,1)} %table.5), custom_call_target="tpu_custom_call" | custom-call | tf_op jit(solution)/shard_map/pallas_call | solution.py:322
  83.2 0.0 collective-permute-done.rows
  83.2 0.0 copy-done.1
  83.2 2.3 %shard_map.64 = f32[2,96]{1,0:T(2,128)S(1)} custom-call(bf16[128,5760]{1,0:T(8,128)(2,1)S(1)} %collective-permute-done.rows, f32[2,4608]{1,0:T(2,128)S(1)} %copy-done, f32[1,4608]{1,0:T(1,128)S(1)} %reshape.53.gain, s32[4,128]{1,0:T(4,128)S(1)} %get-tuple-element.86.places, bf16[384,4608]{1,0:T(8,128)(2,1)S(1)} %copy-done.1), custom_call_target="tpu_custom_call" | custom-call | tf_op jit(solution)/shard_map/pallas_call | solution.py:322
  85.6 11.0 %all_to_all.38 = f32[32,2,96]{2,1,0:T(2,128)S(1)} all-to-all(f32[32,2,96]{2,1,0:T(2,128)S(1)} %bitcast.19), channel_id=1, replica_groups=mesh['dp_0'=4,'dp_1'=4,'dp_2'=2,'vocab'=16] {'dp_0','dp_1','dp_2'}, dimensions={0} | all-to-all | bytes 49152 | tf_op jit(solution)/shard_map/all_to_all | solution.py:26
  96.7 0.6 broadcast_in_dim.11
  97.3 6.8 %all-to-all-start.6 = ((f32[16,2,96]{2,1,0:T(2,128)}), f32[16,2,96]{2,1,0:T(2,128)S(1)}, u32[]{:S(2)}, u32[]{:S(2)}) async-start(f32[16,2,96]{2,1,0:T(2,128)} %broadcast_in_dim.11), calls=%async_computation.6 | async-start | bytes 32768 | tf_op jit(solution)/shard_map/all_to_all | solution.py:26
  104.1 11.4 %all-to-all-done.6 = f32[16,2,96]{2,1,0:T(2,128)S(1)} async-done(((f32[16,2,96]{2,1,0:T(2,128)}), f32[16,2,96]{2,1,0:T(2,128)S(1)}, u32[]{:S(2)}, u32[]{:S(2)}) %all-to-all-start.6) | async-done | bytes 12320 | tf_op jit(solution)/shard_map/all_to_all | solution.py:26
  115.5 0.1 sub.8
  115.6 0.1 dynamic-slice_bitcast_fusion
  115.7 0.7 copy.11
  (7 shorter events, 0.1 us)
Async XLA Ops:
  0.6 14.1 %copy-start = (f32[2,4608]{1,0:T(2,128)S(1)}, f32[2,4608]{1,0:T(2,128)}, u32[]{:S(2)}) copy-start(f32[2,4608]{1,0:T(2,128)} %own_hidden.3) | copy-start | bytes 110596
  0.6 14.1 %copy-start.2 = (s32[64,3]{0,1:T(4,128)S(1)}, s32[64,3]{0,1:T(4,128)}, u32[]{:S(2)}) copy-start(s32[64,3]{0,1:T(4,128)} %param.11) | copy-start | bytes 2308
  0.6 15.7 %copy-start.3 = (f32[4608]{0:T(1024)S(1)}, f32[4608]{0:T(1024)}, u32[]{:S(2)}) copy-start(f32[4608]{0:T(1024)} %param.9) | copy-start | bytes 55300
  3.3 20.9 %all-to-all-start.2 = ((bf16[32,4,1152]{2,1,0:T(4,128)(2,1)}), bf16[32,4,1152]{2,1,0:T(4,128)(2,1)S(1)}, u32[]{:S(2)}, u32[]{:S(2)}) async-start(bf16[32,4,1152]{2,1,0:T(4,128)(2,1)} %shard_map.59), calls=%async_computation.2 | async-start | bytes 589824 | tf_op jit(solution)/shard_map/all_to_all | solution.py:26
  25.5 25.3 %all-to-all-start.3 = ((bf16[16,4,1152]{2,1,0:T(4,128)(2,1)}), bf16[16,4,1152]{2,1,0:T(4,128)(2,1)S(1)}, u32[]{:S(2)}, u32[]{:S(2)}) async-start(bf16[16,4,1152]{2,1,0:T(4,128)(2,1)} %shard_map.61), calls=%async_computation.3 | async-start | bytes 294912 | tf_op jit(solution)/shard_map/all_to_all | solution.py:26
  72.0 11.3 %collective-permute-start = (bf16[128,5760]{1,0:T(8,128)(2,1)S(1)}, bf16[128,5760]{1,0:T(8,128)(2,1)S(1)}, u32[]{:S(2)}, u32[]{:S(2)}) collective-permute-start(bf16[128,5760]{1,0:T(8,128)(2,1)S(1)} %bitcast.11), channel_id=1, source_target_pairs={{0,16},{16,0},{1,17},{17,1},{2,18},{18,2},{3,19},{19,3},{4,20},{20... | collective-permute-start | bytes 4423688 | tf_op jit(solution)/shard_map/ppermute | solution.py:34
  79.1 4.2 %copy-start.1 = (bf16[384,4608]{1,0:T(8,128)(2,1)S(1)}, bf16[384,4608]{1,0:T(8,128)(2,1)}, u32[]{:S(2)}) copy-start(bf16[384,4608]{1,0:T(8,128)(2,1)} %table.5) | copy-start | bytes 10616836
  97.3 18.2 %all-to-all-start.6 = ((f32[16,2,96]{2,1,0:T(2,128)}), f32[16,2,96]{2,1,0:T(2,128)S(1)}, u32[]{:S(2)}, u32[]{:S(2)}) async-start(f32[16,2,96]{2,1,0:T(2,128)} %broadcast_in_dim.11), calls=%async_computation.6 | async-start | bytes 32768 | tf_op jit(solution)/shard_map/all_to_all | solution.py:26
